TPU v7x, 512 devices: a whole 4x8x8 slice. The times are simulated.
512 devices in a mesh: rows: 64 (over y, z), cols: 8 (over x, core).
Axes of the slice: x: 4, y: 8, z: 8, core: 2. Of those that a mesh axis runs over, the one named last changes fastest.
Arguments:
- node_feats: bfloat16 [65536, 128], P(('rows', 'cols')), may hold values from -6 to 6
- weight: bfloat16 [128, 256], replicated, may hold values from -0.5 to 0.5
- att_src: float32 [256], replicated, may hold values from -1.2 to 1.2
- att_dst: float32 [256], replicated, may hold values from -1.2 to 1.2
- out_bias: float32 [256], replicated, may hold values from -3 to 3
- block_src: int32 [512, 8, 32], P(('rows', 'cols')), may hold values from 0 to 63, as said below
- block_count: int32 [512, 8], P(('rows', 'cols')), may hold values from 4 to 32, as said below
- block_bits: int32 [512, 8, 32, 16, 128], P(('rows', 'cols')), may hold values from 0 to 255, as said below
Outputs:
- gat_out: bfloat16 [65536, 256], P(('rows', 'cols'))
Inputs may be any that keep to these rules, and one draw needn't show every extreme that they name: `block_src`: within one block row of one list the 32 slots name distinct source blocks. `block_count`: each entry is 4, 8, 16 or 32; some block row holds 32 in every draw. `block_bits`: each word holds 8 adjacency bits, bit k of word w standing for source column 8 w + k of the block.
All inputs are finite; a program needn't handle non-finite values.
Results may differ from a plain program's by a relative error of at most 0.01.
Values may be sent and summed in bfloat16 or wider, within the bound.
A program may use at most 64 MiB of HBM per device.

v0:
```python
import jax
import jax.numpy as jnp
from jax import lax
from jax.sharding import PartitionSpec as P

HEADS = 4
BLOCK = 128
HEAD_DIM = 64


SLOPE = 0.2


def leaky_relu(raw_score):
    return jnp.where(raw_score > 0, raw_score, SLOPE * raw_score)


def head_scores(projected, attention):
    scaled = projected.astype(jnp.float32) * attention[None, :]
    return jnp.sum(scaled.reshape(projected.shape[0], HEADS, HEAD_DIM), axis=2).T


def unpack_bits(packed):
    shifts = jnp.arange(8, dtype=jnp.int32)
    expanded = jnp.right_shift(packed[..., :, None, :], shifts[:, None]) & 1
    new_shape = packed.shape[:-2] + (packed.shape[-2] * 8, packed.shape[-1])
    return expanded.reshape(new_shape).astype(jnp.float32)


def sparse_rows(gathered, source_scores, target_scores, block_src, block_count, block_bits):
    dest_blocks, link_total = block_src.shape
    group_size = min(16, link_total)
    per_row = link_total // group_size
    src_total = gathered.shape[0] // BLOCK
    values = gathered.reshape(src_total, BLOCK, HEADS, HEAD_DIM)
    source_blocks = source_scores.reshape(HEADS, src_total, BLOCK).transpose(1, 0, 2)
    target_blocks = target_scores.reshape(HEADS, dest_blocks, BLOCK)

    def one_group(running, step_index):
        numerator, denominator = running
        block_row = step_index // per_row
        first_slot = step_index % per_row * group_size
        chosen = lax.dynamic_slice(block_src, (block_row, first_slot), (1, group_size))[0]
        packed = lax.dynamic_slice(
            block_bits, (block_row, first_slot, 0, 0), (1, group_size) + block_bits.shape[2:]
        )[0]
        row_count = lax.dynamic_index_in_dim(block_count, block_row, 0, keepdims=False)
        alive_slots = first_slot + jnp.arange(group_size, dtype=jnp.int32) < row_count
        edge_mask = unpack_bits(packed) * alive_slots.astype(jnp.float32)[:, None, None]
        target = lax.dynamic_index_in_dim(target_blocks, block_row, 1, keepdims=False)
        raw_score = target[None, :, None, :] + source_blocks[chosen][:, :, :, None]
        weights = (jnp.exp(leaky_relu(raw_score)) * edge_mask[:, None]).astype(jnp.bfloat16)
        contrib = jnp.einsum(
            "ghji,gjhk->ihk", weights, values[chosen], preferred_element_type=jnp.float32
        )
        row_total = jnp.sum(weights.astype(jnp.float32), axis=(0, 2))
        numerator = numerator.at[block_row].add(contrib)
        denominator = denominator.at[:, block_row].add(row_total)
        return ((numerator, denominator), None)

    initial = (
        jnp.zeros((dest_blocks, BLOCK, HEADS, HEAD_DIM), jnp.float32),
        jnp.zeros((HEADS, dest_blocks, BLOCK), jnp.float32),
    )
    (numerator, denominator), unused = lax.scan(
        one_group, initial, jnp.arange(dest_blocks * per_row, dtype=jnp.int32)
    )
    return (
        numerator.reshape(dest_blocks * BLOCK, HEADS, HEAD_DIM),
        denominator.reshape(HEADS, dest_blocks * BLOCK),
    )


def shards(node_feats, weight, att_src, att_dst, out_bias, block_src, block_count, block_bits):
    block_src = block_src[0]
    block_count = block_count[0]
    block_bits = block_bits[0]
    node_count = node_feats.shape[0]
    projected = jnp.dot(node_feats, weight, preferred_element_type=jnp.float32).astype(jnp.bfloat16)
    own_source = head_scores(projected, att_src)
    own_target = head_scores(projected, att_dst)
    target_scores = lax.all_gather(own_target, "cols", axis=1, tiled=True)
    dest_rows = target_scores.shape[1]
    gathered = lax.all_gather(projected, "rows", axis=0, tiled=True)
    numerator, denominator = sparse_rows(
        gathered, head_scores(gathered, att_src), target_scores, block_src, block_count, block_bits
    )
    numerator = numerator.reshape(dest_rows, HEADS * HEAD_DIM)
    shares, totals = (
        lax.psum_scatter(numerator, "cols", scatter_dimension=0, tiled=True),
        lax.psum_scatter(denominator.T, "cols", scatter_dimension=0, tiled=True),
    )
    self_round = jnp.exp(leaky_relu(own_target + own_source)).astype(jnp.bfloat16)
    self_weight = lax.optimization_barrier(self_round).astype(jnp.float32).T
    summed = shares.reshape(node_count, HEADS, HEAD_DIM) + self_weight[
        :, :, None
    ] * projected.astype(jnp.float32).reshape(node_count, HEADS, HEAD_DIM)
    blended = (summed / (totals + self_weight)[:, :, None]).reshape(node_count, HEADS * HEAD_DIM)
    return jax.nn.elu(blended + out_bias[None, :]).astype(jnp.bfloat16)


def solution(mesh):
    in_specs = (
        P(("rows", "cols"), None),
        P(),
        P(),
        P(),
        P(),
        P(("rows", "cols"), None, None),
        P(("rows", "cols"), None),
        P(("rows", "cols"), None, None, None, None),
    )
    out_specs = P(("rows", "cols"), None)
    return jax.shard_map(shards, mesh=mesh, in_specs=in_specs, out_specs=out_specs, check_vma=False)
```

profile of v0, /device:TPU:1, one launch (start us, length us, event | category | flops | bytes accessed | tf_op | source)
XLA Modules:
  0.0 550.1 jit_solution(5309863044931015312)
XLA Ops:
  7.4 1.6 convert_multiply_fusion.2
  9.2 17.9 %all_gather.7 = f32[4,1024]{1,0:T(4,128)S(1)} all-gather(f32[4,128]{1,0:T(4,128)S(1)} %bitcast.102), channel_id=1, replica_groups=mesh['rows'=64,'cols'=8] {'cols'}, dimensions={1}, use_global_device_ids=true | all-gather | bytes 18432 | tf_op jit(solution)/shard_map/all_gather | solution.py:82
  27.2 72.0 %all-gather.2.cloned.1.call-done = bf16[8192,256]{1,0:T(8,128)(2,1)} async-done(((bf16[128,256]{1,0:T(8,128)(2,1)}), bf16[8192,256]{1,0:T(8,128)(2,1)}) %all-gather.2.cloned.1.call-update) | async-done | bytes 4194320 | tf_op jit(solution)/shard_map/all_gather | solution.py:84
  99.1 6.0 %convert_multiply_fusion = f32[8192,256]{1,0:T(8,128)} fusion(bf16[8192,256]{1,0:T(8,128)(2,1)} %all-gather.2.cloned.1.call-done, f32[256]{0:T(256)} %param.16), kind=kLoop, calls=%fused_computation.29 | loop fusion | flops 4194304 | bytes 12583936 | tf_op jit(solution)/shard_map/mul | solution.py:19
  105.1 8.9 %copy.30 = f32[8192,256]{0,1:T(8,128)} copy(f32[8192,256]{1,0:T(8,128)} %convert_multiply_fusion) | data formatting | bytes 16777216 | tf_op jit(solution)/shard_map/mul | solution.py:19
  114.0 4.1 bitcast_reduce_fusion
  118.2 12.9 %reshape.196 = bf16[64,128,4,64]{3,2,1,0:T(4,128)(2,1)} reshape(bf16[8192,256]{1,0:T(8,128)(2,1)} %all-gather.2.cloned.1.call-done) | data formatting | bytes 8388608 | tf_op jit(solution)/shard_map/reshape | solution.py:35
  131.1 1.2 broadcast_in_dim.6
  132.3 333.9 %while.16 = (s32[]{:T(128)}, f32[8,128,4,64]{1,3,2,0:T(8,128)}, f32[4,8,128]{2,1,0:T(8,128)S(1)}, s32[16]{0:T(128)S(1)}, s32[8,32]{1,0:T(8,128)}, /*index=5*/bf1...) while((s32[]{:T(128)}, f32[8,128,4,64]{1,3,2,0:T(8,128)}, ...), condition=%wide.region_6.7_spmd, body=%wide.region_2.6_spmd.sunk | while | flops 150013600 | bytes 7172075 | solution.py:65
  136.3 5.7 %gather_fusion.1 = bf16[16,128,4,64]{3,2,1,0:T(4,128)(2,1)S(1)} fusion(bf16[64,128,4,64]{3,2,1,0:T(4,128)(2,1)} %get-tuple-element.311, s32[1024]{0:T(1024)S(1)} %pad_clamp_fusion.2), kind=kCustom, calls=%fused_computation.clone.1 | custom fusion | bytes 2097216 | tf_op jit(solution)/shard_map/while/body/eval_jaxpr/gather | solution.py:54
  142.0 0.9 dynamic-slice_bitcast_fusion.4
  146.0 4.2 fusion.51
  150.2 1.4 convert_reduce_fusion.2
  157.2 5.7 %gather_fusion.1 = bf16[16,128,4,64]{3,2,1,0:T(4,128)(2,1)S(1)} fusion(bf16[64,128,4,64]{3,2,1,0:T(4,128)(2,1)} %get-tuple-element.311, s32[1024]{0:T(1024)S(1)} %pad_clamp_fusion.2), kind=kCustom, calls=%fused_computation.clone.1 | custom fusion | bytes 2097216 | tf_op jit(solution)/shard_map/while/body/eval_jaxpr/gather | solution.py:54
  166.9 4.2 fusion.51
  171.1 1.4 convert_reduce_fusion.2
  178.0 5.7 %gather_fusion.1 = bf16[16,128,4,64]{3,2,1,0:T(4,128)(2,1)S(1)} fusion(bf16[64,128,4,64]{3,2,1,0:T(4,128)(2,1)} %get-tuple-element.311, s32[1024]{0:T(1024)S(1)} %pad_clamp_fusion.2), kind=kCustom, calls=%fused_computation.clone.1 | custom fusion | bytes 2097216 | tf_op jit(solution)/shard_map/while/body/eval_jaxpr/gather | solution.py:54
  187.8 4.2 fusion.51
  191.9 1.4 convert_reduce_fusion.2
  198.9 5.7 %gather_fusion.1 = bf16[16,128,4,64]{3,2,1,0:T(4,128)(2,1)S(1)} fusion(bf16[64,128,4,64]{3,2,1,0:T(4,128)(2,1)} %get-tuple-element.311, s32[1024]{0:T(1024)S(1)} %pad_clamp_fusion.2), kind=kCustom, calls=%fused_computation.clone.1 | custom fusion | bytes 2097216 | tf_op jit(solution)/shard_map/while/body/eval_jaxpr/gather | solution.py:54
  208.6 4.2 fusion.51
  212.8 1.4 convert_reduce_fusion.2
  219.7 5.7 %gather_fusion.1 = bf16[16,128,4,64]{3,2,1,0:T(4,128)(2,1)S(1)} fusion(bf16[64,128,4,64]{3,2,1,0:T(4,128)(2,1)} %get-tuple-element.311, s32[1024]{0:T(1024)S(1)} %pad_clamp_fusion.2), kind=kCustom, calls=%fused_computation.clone.1 | custom fusion | bytes 2097216 | tf_op jit(solution)/shard_map/while/body/eval_jaxpr/gather | solution.py:54
  229.5 4.2 fusion.51
  233.7 1.4 convert_reduce_fusion.2
  240.6 5.7 %gather_fusion.1 = bf16[16,128,4,64]{3,2,1,0:T(4,128)(2,1)S(1)} fusion(bf16[64,128,4,64]{3,2,1,0:T(4,128)(2,1)} %get-tuple-element.311, s32[1024]{0:T(1024)S(1)} %pad_clamp_fusion.2), kind=kCustom, calls=%fused_computation.clone.1 | custom fusion | bytes 2097216 | tf_op jit(solution)/shard_map/while/body/eval_jaxpr/gather | solution.py:54
  250.4 4.2 fusion.51
  254.6 1.4 convert_reduce_fusion.2
  261.5 5.7 %gather_fusion.1 = bf16[16,128,4,64]{3,2,1,0:T(4,128)(2,1)S(1)} fusion(bf16[64,128,4,64]{3,2,1,0:T(4,128)(2,1)} %get-tuple-element.311, s32[1024]{0:T(1024)S(1)} %pad_clamp_fusion.2), kind=kCustom, calls=%fused_computation.clone.1 | custom fusion | bytes 2097216 | tf_op jit(solution)/shard_map/while/body/eval_jaxpr/gather | solution.py:54
  271.2 4.2 fusion.51
  275.4 1.4 convert_reduce_fusion.2
  282.4 5.7 %gather_fusion.1 = bf16[16,128,4,64]{3,2,1,0:T(4,128)(2,1)S(1)} fusion(bf16[64,128,4,64]{3,2,1,0:T(4,128)(2,1)} %get-tuple-element.311, s32[1024]{0:T(1024)S(1)} %pad_clamp_fusion.2), kind=kCustom, calls=%fused_computation.clone.1 | custom fusion | bytes 2097216 | tf_op jit(solution)/shard_map/while/body/eval_jaxpr/gather | solution.py:54
  292.1 4.2 fusion.51
  296.3 1.4 convert_reduce_fusion.2
  303.2 5.7 %gather_fusion.1 = bf16[16,128,4,64]{3,2,1,0:T(4,128)(2,1)S(1)} fusion(bf16[64,128,4,64]{3,2,1,0:T(4,128)(2,1)} %get-tuple-element.311, s32[1024]{0:T(1024)S(1)} %pad_clamp_fusion.2), kind=kCustom, calls=%fused_computation.clone.1 | custom fusion | bytes 2097216 | tf_op jit(solution)/shard_map/while/body/eval_jaxpr/gather | solution.py:54
  313.0 4.2 fusion.51
  317.1 1.4 convert_reduce_fusion.2
  324.1 5.7 %gather_fusion.1 = bf16[16,128,4,64]{3,2,1,0:T(4,128)(2,1)S(1)} fusion(bf16[64,128,4,64]{3,2,1,0:T(4,128)(2,1)} %get-tuple-element.311, s32[1024]{0:T(1024)S(1)} %pad_clamp_fusion.2), kind=kCustom, calls=%fused_computation.clone.1 | custom fusion | bytes 2097216 | tf_op jit(solution)/shard_map/while/body/eval_jaxpr/gather | solution.py:54
  333.8 4.2 fusion.51
  338.0 1.4 convert_reduce_fusion.2
  345.0 5.7 %gather_fusion.1 = bf16[16,128,4,64]{3,2,1,0:T(4,128)(2,1)S(1)} fusion(bf16[64,128,4,64]{3,2,1,0:T(4,128)(2,1)} %get-tuple-element.311, s32[1024]{0:T(1024)S(1)} %pad_clamp_fusion.2), kind=kCustom, calls=%fused_computation.clone.1 | custom fusion | bytes 2097216 | tf_op jit(solution)/shard_map/while/body/eval_jaxpr/gather | solution.py:54
  354.7 4.2 fusion.51
  358.9 1.4 convert_reduce_fusion.2
  365.8 5.7 %gather_fusion.1 = bf16[16,128,4,64]{3,2,1,0:T(4,128)(2,1)S(1)} fusion(bf16[64,128,4,64]{3,2,1,0:T(4,128)(2,1)} %get-tuple-element.311, s32[1024]{0:T(1024)S(1)} %pad_clamp_fusion.2), kind=kCustom, calls=%fused_computation.clone.1 | custom fusion | bytes 2097216 | tf_op jit(solution)/shard_map/while/body/eval_jaxpr/gather | solution.py:54
  375.6 4.2 fusion.51
  379.8 1.4 convert_reduce_fusion.2
  386.7 5.7 %gather_fusion.1 = bf16[16,128,4,64]{3,2,1,0:T(4,128)(2,1)S(1)} fusion(bf16[64,128,4,64]{3,2,1,0:T(4,128)(2,1)} %get-tuple-element.311, s32[1024]{0:T(1024)S(1)} %pad_clamp_fusion.2), kind=kCustom, calls=%fused_computation.clone.1 | custom fusion | bytes 2097216 | tf_op jit(solution)/shard_map/while/body/eval_jaxpr/gather | solution.py:54
  396.5 4.2 fusion.51
  400.7 1.4 convert_reduce_fusion.2
  407.6 5.7 %gather_fusion.1 = bf16[16,128,4,64]{3,2,1,0:T(4,128)(2,1)S(1)} fusion(bf16[64,128,4,64]{3,2,1,0:T(4,128)(2,1)} %get-tuple-element.311, s32[1024]{0:T(1024)S(1)} %pad_clamp_fusion.2), kind=kCustom, calls=%fused_computation.clone.1 | custom fusion | bytes 2097216 | tf_op jit(solution)/shard_map/while/body/eval_jaxpr/gather | solution.py:54
  417.3 4.2 fusion.51
  421.5 1.4 convert_reduce_fusion.2
  428.5 5.7 %gather_fusion.1 = bf16[16,128,4,64]{3,2,1,0:T(4,128)(2,1)S(1)} fusion(bf16[64,128,4,64]{3,2,1,0:T(4,128)(2,1)} %get-tuple-element.311, s32[1024]{0:T(1024)S(1)} %pad_clamp_fusion.2), kind=kCustom, calls=%fused_computation.clone.1 | custom fusion | bytes 2097216 | tf_op jit(solution)/shard_map/while/body/eval_jaxpr/gather | solution.py:54
  438.2 4.2 fusion.51
  442.4 1.4 convert_reduce_fusion.2
  449.3 5.7 %gather_fusion.1 = bf16[16,128,4,64]{3,2,1,0:T(4,128)(2,1)S(1)} fusion(bf16[64,128,4,64]{3,2,1,0:T(4,128)(2,1)} %get-tuple-element.311, s32[1024]{0:T(1024)S(1)} %pad_clamp_fusion.2), kind=kCustom, calls=%fused_computation.clone.1 | custom fusion | bytes 2097216 | tf_op jit(solution)/shard_map/while/body/eval_jaxpr/gather | solution.py:54
  459.1 4.2 fusion.51
  463.3 1.4 convert_reduce_fusion.2
  466.3 1.1 copy.42
  467.4 1.9 copy.41
  469.3 2.1 reshape.197
  471.6 31.2 %reduce-scatter.7.cloned.1.call-done = f32[128,4]{1,0:T(8,128)} async-done(((f32[1024,4]{1,0:T(8,128)}), f32[128,4]{1,0:T(8,128)}) %reduce-scatter.7.cloned.1.call-update) | async-done | bytes 2064
  503.8 38.1 %reduce-scatter.5.cloned.1.call-done = f32[128,256]{1,0:T(8,128)} async-done(((f32[1024,256]{1,0:T(8,128)}), f32[128,256]{1,0:T(8,128)}) %reduce-scatter.5.cloned.1.call-update) | async-done | bytes 131088 | tf_op jit(solution)/shard_map/reduce_scatter | solution.py:90
  541.9 1.6 fusion.36
  (289 shorter events, 111.4 us)
Async XLA Ops:
  6.5 0.8 copy-start
  6.5 92.6 %all-gather.2.cloned.1.call-start = ((), (), s32[]{:S(2)}) async-start(), calls=%async_computation.2 | async-start | bytes 4259840 | tf_op jit(solution)/shard_map/all_gather | solution.py:84
  9.0 493.8 %reduce-scatter.7.cloned.1.call-start = ((), (), s32[]{:S(2)}) async-start(), calls=%async_computation.4 | async-start | bytes 589824
  118.2 14.1 %copy-start.2 = (s32[4]{0:T(128)S(1)}, s32[4]{0:T(128)}, u32[]{:S(2)}) copy-start(s32[4]{0:T(128)} %constant.146.clone.1) | copy-start | bytes 52
  118.2 14.1 %copy-start.3 = (s32[3]{0:T(128)S(1)}, s32[3]{0:T(128)}, u32[]{:S(2)}) copy-start(s32[3]{0:T(128)} %constant.154.clone.1) | copy-start | bytes 40
  118.2 14.1 %copy-start.5 = (s32[1,8]{1,0:T(1,128)S(1)}, s32[1,8]{1,0:T(1,128)}, u32[]{:S(2)}) copy-start(s32[1,8]{1,0:T(1,128)} %param.20) | copy-start | bytes 100
  467.3 74.6 %copy-start.1 = (bf16[128,256]{1,0:T(8,128)(2,1)S(1)}, bf16[128,256]{1,0:T(8,128)(2,1)}, u32[]{:S(2)}) copy-start(bf16[128,256]{1,0:T(8,128)(2,1)} %get-tuple-element.202) | copy-start | bytes 196612
  467.4 74.6 %copy-start.4 = (f32[256]{0:T(256)S(1)}, f32[256]{0:T(256)}, u32[]{:S(2)}) copy-start(f32[256]{0:T(256)} %param.18) | copy-start | bytes 3076
  467.4 74.6 %reduce-scatter.5.cloned.1.call-start = ((), (), s32[]{:S(2)}) async-start(), calls=%async_computation.3 | async-start | bytes 1179648 | tf_op jit(solution)/shard_map/reduce_scatter | solution.py:90
Sparse Core Ops, SparseCore 0:
  10.4 88.7 all-gather.1
  467.5 35.2 reduce-scatter.6
  505.8 36.0 reduce-scatter.4
where the time goes:
time: 554 us; the launch traced here: 550 us
  local copies, waits for them, and re-layouts  169 us (31%)
  waiting for transfers between devices  141 us (25%)
  other arithmetic  97.6 us (18%)
  matrix products  68.6 us (12%)
  loops' own time  42 us (8%)
  blocking collectives  17.9 us (3%)
  between operations  13.3 us (2%)
    gather x16, local copies, waits for them, and re-layouts, one_group(): values[chosen]  91.8 us
    all_gather x1, waiting for transfers between devices, shards(): gathered = lax.all_gather(projected, 'rows', axis=0, tiled=True)  72 us
    dot_general x16, matrix products, one_group(): jnp.einsum('ghji,gjhk->ihk', weights, values[chosen], preferred_element_t...  67 us
    another operation x1, loops' own time, sparse_rows(): lax.scan(one_group, initial, jnp.arange(dest_blocks * per_row, dtype=jnp....  42 us
    reduce_scatter x1, waiting for transfers between devices, shards(): lax.psum_scatter(numerator, 'cols', scatter_dimension=0, tiled=True)  38.1 us
    another operation x48, other arithmetic  36 us
    unnamed x4, waiting for transfers between devices  31.2 us
    reduce_sum x16, other arithmetic, one_group(): row_total = jnp.sum(weights.astype(jnp.float32), axis=(0, 2))  23.2 us
  transfers between devices with their start and end apart: 3, of which 3 were waited for; matrix products, arithmetic and copies ran while one was open for 1% of the time, Pallas kernels for 0%

commit v1 on v0

v1 whole, which is shorter than its diff:
```python
import functools
import math

import jax
import jax.numpy as jnp
from jax import lax
from jax.experimental import pallas as pl
from jax.experimental.pallas import tpu as pltpu
from jax.sharding import PartitionSpec as P

HEADS = 4
BLOCK = 128
HEAD_DIM = 64
HID = HEADS * HEAD_DIM
HALF = BLOCK // 2
SLOPE = 0.2
RISE = 1.0 - SLOPE
SAFE = 100.0
V_ROWS = 80
P_ROWS = HID + 16
GROUP = 4
MESH = pl.DeviceIdType.MESH
F32 = jnp.float32
BF16 = jnp.bfloat16
NT = (((1,), (1,)), ((), ()))
TN = (((0,), (0,)), ((), ()))


def leaky_relu(raw):
    return jnp.where(raw > 0, raw, SLOPE * raw)


def attention_rows(att):
    high = att.astype(BF16).astype(F32)
    middle = (att - high).astype(BF16).astype(F32)
    low = att - high - middle
    row = lax.broadcasted_iota(jnp.int32, (32, HID), 0)
    column = lax.broadcasted_iota(jnp.int32, (32, HID), 1)
    piece = jnp.where(row < 8, high, jnp.where(row < 16, middle, low))
    return jnp.where((row % 8 == column // HEAD_DIM) & (row < 24), piece, 0.0).astype(BF16)


def scores_of(rows, projected_t):
    parts = jnp.dot(rows, projected_t, preferred_element_type=F32)
    return parts[0:8] + parts[8:16] + parts[16:24]


def project_t(weight_t, feats):
    return lax.dot_general(weight_t, feats, NT, preferred_element_type=F32).astype(BF16)


def transposed(weight):
    return jnp.transpose(weight.astype(F32)).astype(BF16)


def gather_kernel(side, cols, x_ref, w_ref, adst_ref, ga_ref, gb_ref, d_ref, xp, dme,
                  local_sem, d_send, d_recv, one_send, one_recv, two_send, two_recv):
    r, c = lax.axis_index("rows"), lax.axis_index("cols")
    y, z = r // side, r % side

    def at(yy, zz):
        return (yy * side + zz, c)

    barrier = pltpu.get_barrier_semaphore()
    for k in range(1, side):
        pl.semaphore_signal(barrier, inc=1, device_id=at(y, (z + k) % side), device_id_type=MESH)
        pl.semaphore_signal(barrier, inc=1, device_id=at((y + k) % side, z), device_id_type=MESH)
    for k in range(1, cols):
        pl.semaphore_signal(barrier, inc=1, device_id=(r, (c + k) % cols), device_id_type=MESH)

    place = lax.broadcasted_iota(jnp.int32, (BLOCK, BLOCK), 0)
    node = lax.broadcasted_iota(jnp.int32, (BLOCK, BLOCK), 1)
    order = jnp.where(node == 8 * (place % 16) + place // 16, 1.0, 0.0).astype(BF16)
    xp[...] = jnp.dot(order, x_ref[...], preferred_element_type=F32).astype(BF16)
    dme[...] = scores_of(attention_rows(adst_ref[...]), project_t(transposed(w_ref[...]), x_ref[...]))
    pl.semaphore_wait(barrier, 2 * (side - 1) + cols - 1)

    first = []
    for k in range(1, side):
        first.append(pltpu.make_async_remote_copy(
            xp.at[pl.ds(0, HALF)], ga_ref.at[y, z], one_send.at[0, k - 1], one_recv.at[0, k - 1],
            device_id=at(y, (z + k) % side), device_id_type=MESH))
        first.append(pltpu.make_async_remote_copy(
            xp.at[pl.ds(HALF, HALF)], gb_ref.at[z, y], one_send.at[1, k - 1], one_recv.at[1, k - 1],
            device_id=at((y + k) % side, z), device_id_type=MESH))
    for copy in first:
        copy.start()
    own = [
        pltpu.make_async_copy(xp.at[pl.ds(0, HALF)], ga_ref.at[y, z], local_sem.at[0]),
        pltpu.make_async_copy(xp.at[pl.ds(HALF, HALF)], gb_ref.at[z, y], local_sem.at[1]),
        pltpu.make_async_copy(dme, d_ref.at[c], local_sem.at[2]),
    ]
    for copy in own:
        copy.start()
    scores = []
    for k in range(1, cols):
        scores.append(pltpu.make_async_remote_copy(
            dme, d_ref.at[c], d_send.at[k - 1], d_recv.at[k - 1],
            device_id=(r, (c + k) % cols), device_id_type=MESH))
        scores[-1].start()
    for copy in own:
        copy.wait()
    for copy in first:
        copy.wait_recv()

    sub = side // 2
    half_way = side // 2

    def second(half, way, step, part):
        buffer, place = (ga_ref, y) if half == 0 else (gb_ref, z)
        if way == 0:
            block, target = (place - step + 1 + side) % side, (place + 1) % side
        else:
            block, target = (place + step - 1) % side, (place + side - 1) % side
        ref = buffer.at[block, pl.ds(part * sub, sub)]
        return pltpu.make_async_remote_copy(
            ref, ref, two_send.at[half, way, step - 1, part], two_recv.at[half, way, step - 1, part],
            device_id=at(target, z) if half == 0 else at(y, target), device_id_type=MESH)

    lanes = [(half, way) for half in range(2) for way in range(2)]
    inflight = {}
    for step in range(1, half_way + 1):
        for part in range(2):
            for half, way in lanes:
                if step > 1:
                    inflight[half, way, step - 1, part].wait_recv()
                if step < half_way or part == way:
                    inflight[half, way, step, part] = second(half, way, step, part)
                    inflight[half, way, step, part].start()
    for half, way in lanes:
        inflight[half, way, half_way, way].wait_recv()
    for copy in scores:
        copy.wait_recv()
    for copy in first + scores + list(inflight.values()):
        copy.wait_send()


def gather(side, cols, node_feats, weight, att_dst):
    vmem = pl.BlockSpec(memory_space=pltpu.VMEM)
    hbm = pl.BlockSpec(memory_space=pl.ANY)
    dma = pltpu.SemaphoreType.DMA
    return pl.pallas_call(
        functools.partial(gather_kernel, side, cols),
        out_shape=(
            jax.ShapeDtypeStruct((side, side, HALF, BLOCK), BF16),
            jax.ShapeDtypeStruct((side, side, HALF, BLOCK), BF16),
            jax.ShapeDtypeStruct((cols, 8, BLOCK), F32),
        ),
        in_specs=[vmem, vmem, vmem],
        out_specs=(hbm, hbm, hbm),
        scratch_shapes=[
            pltpu.VMEM((BLOCK, BLOCK), BF16),
            pltpu.VMEM((8, BLOCK), F32),
            dma((3,)), dma((cols - 1,)), dma((cols - 1,)),
            dma((2, side - 1)), dma((2, side - 1)),
            dma((2, 2, side // 2, 2)), dma((2, 2, side // 2, 2)),
        ],
        compiler_params=pltpu.CompilerParams(collective_id=0, has_side_effects=True),
        name="gather_features",
    )(node_feats, weight, att_dst)


def aggregate_kernel(side, src_ref, count_ref, bits_ref, ga_ref, gb_ref, d_ref, w_ref, asrc_ref, p_ref,
                     vt, eb, st, acc):
    dest = d_ref.shape[0]
    weight_t = transposed(w_ref[...])
    rows = attention_rows(asrc_ref[...])
    ones_row = jnp.where(lax.broadcasted_iota(jnp.int32, (16, BLOCK), 0) == 0, 1.0, 0.0)
    spread_row = lax.broadcasted_iota(jnp.int32, (16, HEADS * BLOCK), 0)
    spread_col = lax.broadcasted_iota(jnp.int32, (16, HEADS * BLOCK), 1)
    spread = jnp.where(spread_row == spread_col // BLOCK, 1.0, 0.0).astype(BF16)

    def blocks_of(y):
        pieces = []
        for z in range(side):
            pieces += [ga_ref[y, z], gb_ref[z, y]]
        feats = jnp.concatenate(pieces, axis=0)
        projected = project_t(weight_t, feats)
        return projected, scores_of(rows, projected)

    def prepare(y, largest):
        projected, score = blocks_of(y)
        scale = jnp.exp(SLOPE * score)
        rise = jnp.exp(RISE * score)
        rise = jnp.concatenate([rise, jnp.zeros_like(rise)], axis=0).astype(BF16)
        for z in range(side):
            at = slice(z * BLOCK, (z + 1) * BLOCK)
            block = y * side + z
            for h in range(HEADS):
                c_row = scale[h:h + 1, at]
                values = projected[h * HEAD_DIM:(h + 1) * HEAD_DIM, at].astype(F32) * c_row
                vt[block, h] = jnp.concatenate([values, ones_row * c_row], axis=0).astype(BF16)
            source = lax.dot_general(rise[:, at], spread, TN, preferred_element_type=F32).astype(BF16)
            for h in range(HEADS):
                eb[block, pl.ds(h * BLOCK, BLOCK)] = source[:, h * BLOCK:(h + 1) * BLOCK]
        return jnp.maximum(largest, jnp.abs(score))

    largest = lax.fori_loop(0, side, prepare, jnp.zeros((8, side * BLOCK), F32))
    largest = jnp.maximum(jnp.max(largest), jnp.max(jnp.abs(d_ref[...])))
    safe = largest <= SAFE

    def run(weights_of, finish):
        def one_row(d, carry):
            acc[...] = jnp.zeros_like(acc)
            own = d_ref[d]

            def one_group(g, inner):
                slots = [g * GROUP + i for i in range(GROUP)]
                blocks = [src_ref[d, slot] for slot in slots]
                per_slot = [weights_of(d, slot, block, own) for slot, block in zip(slots, blocks)]
                for h in range(HEADS):
                    edge = jnp.concatenate([piece for one in per_slot for piece in one[h]], axis=0)
                    values = jnp.concatenate([vt[block, h] for block in blocks], axis=1)
                    acc[h] += jnp.dot(values, edge, preferred_element_type=F32)
                return inner

            lax.fori_loop(0, count_ref[d] // GROUP, one_group, 0)
            finish(d, own)
            return carry

        lax.fori_loop(0, dest, one_row, 0)

    def store(d, factor):
        denominators = []
        for h in range(HEADS):
            scaled = acc[h] * factor[h:h + 1, :]
            p_ref[d, pl.ds(h * HEAD_DIM, HEAD_DIM)] = scaled[:HEAD_DIM].astype(BF16)
            denominators.append(scaled[HEAD_DIM:HEAD_DIM + 1])
        denominators.append(jnp.zeros((16 - HEADS, BLOCK), F32))
        p_ref[d, pl.ds(HID, 16)] = jnp.concatenate(denominators, axis=0).astype(BF16)

    def factored(d, slot, block, own):
        words = bits_ref[d, slot].astype(jnp.int16)
        live = [(words & (1 << k)) != 0 for k in range(8)]
        reach = jnp.exp(RISE * own).astype(BF16)
        one = jnp.ones((16, BLOCK), BF16)
        none = jnp.zeros((16, BLOCK), BF16)
        result = []
        for h in range(HEADS):
            target = jnp.broadcast_to(reach[h:h + 1, :], (16, BLOCK))
            pieces = []
            for k in range(8):
                source = eb[block, pl.ds(h * BLOCK + k * 16, 16)]
                pieces.append(jnp.where(live[k], jnp.maximum(source * target, one), none))
            result.append(pieces)
        return result

    @pl.when(safe)
    def _():
        run(factored, lambda d, own: store(d, jnp.exp(SLOPE * own)))

    def direct(d, slot, block, own):
        words = bits_ref[d, slot]
        live = jnp.concatenate([jnp.right_shift(words, k) & 1 for k in range(8)], axis=0) != 0
        result = []
        for h in range(HEADS):
            raw = st[block, :, pl.ds(h, 1)] + own[h:h + 1, :]
            result.append([jnp.where(live, jnp.exp(leaky_relu(raw)), 0.0).astype(BF16)])
        return result

    @pl.when(jnp.logical_not(safe))
    def _():
        def prepare_direct(y, carry):
            projected, score = blocks_of(y)
            for z in range(side):
                at = slice(z * BLOCK, (z + 1) * BLOCK)
                block = y * side + z
                for h in range(HEADS):
                    values = projected[h * HEAD_DIM:(h + 1) * HEAD_DIM, at].astype(F32)
                    vt[block, h] = jnp.concatenate([values, ones_row], axis=0).astype(BF16)
                st[block] = jnp.transpose(score[:, at])
            return carry

        lax.fori_loop(0, side, prepare_direct, 0)
        run(direct, lambda d, own: store(d, jnp.ones_like(own)))


def aggregate(side, block_src, block_count, block_bits, ga, gb, target_scores, weight, att_src):
    vmem = pl.BlockSpec(memory_space=pltpu.VMEM)
    smem = pl.BlockSpec(memory_space=pltpu.SMEM)
    dest = block_src.shape[0]
    sources = side * side
    return pl.pallas_call(
        functools.partial(aggregate_kernel, side),
        out_shape=jax.ShapeDtypeStruct((dest, P_ROWS, BLOCK), BF16),
        in_specs=[smem, smem, vmem, vmem, vmem, vmem, vmem, vmem],
        out_specs=vmem,
        scratch_shapes=[
            pltpu.VMEM((sources, HEADS, V_ROWS, BLOCK), BF16),
            pltpu.VMEM((sources, HEADS * BLOCK, BLOCK), BF16),
            pltpu.VMEM((sources, BLOCK, 8), F32),
            pltpu.VMEM((HEADS, V_ROWS, BLOCK), F32),
        ],
        compiler_params=pltpu.CompilerParams(vmem_limit_bytes=40 * 1024 * 1024),
        name="aggregate_edges",
    )(block_src, block_count, block_bits, ga, gb, target_scores, weight, att_src)


def combine_kernel(cols, p_ref, x_ref, w_ref, asrc_ref, adst_ref, bias_ref, out_ref, land, send, recv):
    r, c = lax.axis_index("rows"), lax.axis_index("cols")
    barrier = pltpu.get_barrier_semaphore()
    for k in range(1, cols):
        pl.semaphore_signal(barrier, inc=1, device_id=(r, (c + k) % cols), device_id_type=MESH)
    pl.semaphore_wait(barrier, cols - 1)
    copies = []
    for k in range(1, cols):
        peer = (c + k) % cols
        copies.append(pltpu.make_async_remote_copy(
            p_ref.at[peer], land.at[k - 1], send.at[k - 1], recv.at[k - 1],
            device_id=(r, peer), device_id_type=MESH))
        copies[-1].start()

    projected = project_t(transposed(w_ref[...]), x_ref[...])
    raw = scores_of(attention_rows(asrc_ref[...]), projected) + scores_of(attention_rows(adst_ref[...]), projected)
    self_weight = jnp.exp(leaky_relu(raw)).astype(BF16).astype(F32)
    own = p_ref[c].astype(F32)
    numerator = [
        own[h * HEAD_DIM:(h + 1) * HEAD_DIM]
        + projected[h * HEAD_DIM:(h + 1) * HEAD_DIM].astype(F32) * self_weight[h:h + 1]
        for h in range(HEADS)
    ]
    total = jnp.concatenate(numerator, axis=0)
    denominator = own[HID:HID + 8] + self_weight
    for k, copy in enumerate(copies):
        copy.wait_recv()
        total = total + land[k, pl.ds(0, HID)].astype(F32)
        denominator = denominator + land[k, pl.ds(HID, 16)].astype(F32)[:8]
    blended = jnp.concatenate(
        [total[h * HEAD_DIM:(h + 1) * HEAD_DIM] / denominator[h:h + 1] for h in range(HEADS)], axis=0)
    value = jnp.transpose(blended) + bias_ref[...]
    out_ref[...] = jnp.where(value > 0, value, jnp.exp(jnp.minimum(value, 0.0)) - 1.0).astype(BF16)
    for copy in copies:
        copy.wait_send()


def combine(cols, partials, node_feats, weight, att_src, att_dst, out_bias):
    vmem = pl.BlockSpec(memory_space=pltpu.VMEM)
    return pl.pallas_call(
        functools.partial(combine_kernel, cols),
        out_shape=jax.ShapeDtypeStruct((BLOCK, HID), BF16),
        in_specs=[vmem] * 6,
        out_specs=vmem,
        scratch_shapes=[
            pltpu.VMEM((cols - 1, P_ROWS, BLOCK), BF16),
            pltpu.SemaphoreType.DMA((cols - 1,)),
            pltpu.SemaphoreType.DMA((cols - 1,)),
        ],
        compiler_params=pltpu.CompilerParams(collective_id=1, has_side_effects=True),
        name="combine_partials",
    )(partials, node_feats, weight, att_src, att_dst, out_bias)


def shards(side, cols, node_feats, weight, att_src, att_dst, out_bias, block_src, block_count, block_bits):
    att_src, att_dst, out_bias = (v.reshape(1, HID) for v in (att_src, att_dst, out_bias))
    ga, gb, target_scores = gather(side, cols, node_feats, weight, att_dst)
    partials = aggregate(
        side, block_src[0], block_count[0], block_bits[0], ga, gb, target_scores, weight, att_src)
    return combine(cols, partials, node_feats, weight, att_src, att_dst, out_bias)


def solution(mesh):
    side = math.isqrt(mesh.shape["rows"])
    cols = mesh.shape["cols"]
    in_specs = (
        P(("rows", "cols"), None),
        P(),
        P(),
        P(),
        P(),
        P(("rows", "cols"), None, None),
        P(("rows", "cols"), None),
        P(("rows", "cols"), None, None, None, None),
    )
    return jax.shard_map(
        functools.partial(shards, side, cols), mesh=mesh, in_specs=in_specs,
        out_specs=P(("rows", "cols"), None), check_vma=False)
```

time: 554 us -> 84.4 us (0.15)
  local copies, waits for them, and re-layouts: 169 us -> 9.92 us
  waiting for transfers between devices: 141 us -> 0 us
  other arithmetic: 97.6 us -> 0 us
  Pallas kernels: 0 us -> 73.9 us
  matrix products: 68.6 us -> 0 us
  loops' own time: 42 us -> 0 us
  blocking collectives: 17.9 us -> 0 us
  between operations: 13.3 us -> 0.05 us
    gather x48 -> x0, local copies, waits for them, and re-layouts: 101 us -> none  [the longest x16 91.8 us: one_group(): values[chosen]]
    pallas_call x0 -> x3, Pallas kernels: none -> 73.9 us  [the longest x1 37.8 us: gather(): pl.pallas_call(functools.partial(gather_kernel, side, cols), out_shape=(j...]
    all_gather x1 -> x0, waiting for transfers between devices: 72 us -> none  [shards(): gathered = lax.all_gather(projected, 'rows', axis=0, tiled=True)]
    dot_general x17 -> x0, matrix products: 68.6 us -> none  [the longest x16 67 us: one_group(): jnp.einsum('ghji,gjhk->ihk', weights, values[chosen], preferred_element_t...]
    another operation x1 -> x0, loops' own time: 42 us -> none  [sparse_rows(): lax.scan(one_group, initial, jnp.arange(dest_blocks * per_row, dtype=jnp....]
    reduce_scatter x1 -> x0, waiting for transfers between devices: 38.1 us -> none  [shards(): lax.psum_scatter(numerator, 'cols', scatter_dimension=0, tiled=True)]
    another operation x48 -> x0, other arithmetic: 36 us -> none
    unnamed x4 -> x0, waiting for transfers between devices: 31.2 us -> none
  transfers between devices with their start and end apart: 3 -> 0, of which waited for: 3 -> 0; matrix products, arithmetic and copies ran while one was open for 1% -> 0% of each run, Pallas kernels for 0% -> 0%
where the time goes in v1:
time: 84.4 us; the launch traced here: 83.9 us
  Pallas kernels  73.9 us (88%)
  local copies, waits for them, and re-layouts  9.92 us (12%)
    pallas_call x1, Pallas kernels, gather(): pl.pallas_call(functools.partial(gather_kernel, side, cols), out_shape=(j...  37.8 us
    pallas_call x1, Pallas kernels, combine(): pl.pallas_call(functools.partial(combine_kernel, cols), out_shape=jax.Sha...  19.2 us
    pallas_call x1, Pallas kernels, aggregate(): pl.pallas_call(functools.partial(aggregate_kernel, side), out_shape=jax.S...  16.9 us
    unnamed x19, local copies, waits for them, and re-layouts  9.92 us

profile of v1, /device:TPU:1, one launch (start us, length us, event | category | flops | bytes accessed | tf_op | source)
XLA Modules:
  0.0 83.9 jit_solution(9516452189045455225)
XLA Ops:
  0.0 37.8 %gather_features.1 = (bf16[8,8,64,128]{3,2,1,0:T(8,128)(2,1)}, bf16[8,8,64,128]{3,2,1,0:T(8,128)(2,1)}, f32[8,8,128]{2,1,0:T(8,128)}) custom-call(bf16[128,128]{1,0:T(8,128)(2,1)} %x_ref.3, bf16[128,256]{1,0:T(8,128)(2,1)} %w_ref.5, f32[1,256]{1,0:T(1,128)} %bitcast.11), custom_call_target="tpu_custom_call" | custom-call | tf_op jit(solution)/shard_map/gather_features/pallas_call | solution.py:142
  37.8 0.0 copy-start.1
  37.8 1.6 %copy-done.1 = s32[1,8,32,16,128]{4,3,2,1,0:T(8,128)S(1)} copy-done((s32[1,8,32,16,128]{4,3,2,1,0:T(8,128)S(1)}, s32[1,8,32,16,128]{4,3,2,1,0:T(8,128)}, u32[]{:S(2)}) %copy-start.1) | copy-done | bytes 2097176
  39.4 0.0 copy-start.2
  39.4 1.2 %copy-done.2 = bf16[8,8,64,128]{3,2,1,0:T(8,128)(2,1)S(1)} copy-done((bf16[8,8,64,128]{3,2,1,0:T(8,128)(2,1)S(1)}, bf16[8,8,64,128]{3,2,1,0:T(8,128)(2,1)}, u32[]{:S(2)}) %copy-start.2) | copy-done | bytes 1048600
  40.6 0.0 copy-start.3
  40.6 1.2 %copy-done.3 = bf16[8,8,64,128]{3,2,1,0:T(8,128)(2,1)S(1)} copy-done((bf16[8,8,64,128]{3,2,1,0:T(8,128)(2,1)S(1)}, bf16[8,8,64,128]{3,2,1,0:T(8,128)(2,1)}, u32[]{:S(2)}) %copy-start.3) | copy-done | bytes 1048600
  41.9 0.0 copy-start.4
  41.9 0.8 copy-done.4
  42.7 0.0 copy-start.5
  42.7 0.8 copy-done.5
  43.5 0.0 copy-start.6
  43.5 0.7 copy-done.6
  44.1 0.0 copy-start.7
  44.2 0.7 copy-done.7
  44.8 0.0 copy-start.8
  44.8 0.7 copy-done.8
  45.5 16.9 %aggregate_edges.1.p_ref = bf16[8,272,128]{2,1,0:T(8,128)(2,1)S(1)} custom-call(s32[8,32]{1,0:T(8,128)S(1)} %bitcast.7, s32[8]{0:T(128)S(1)} %bitcast.10, s32[8,32,16,128]{3,2,1,0:T(8,128)S(1)} %bitcast.6, bf16[8,8,64,128]{3,2,1,0:T(8,128)(2,1)S(1)} %copy-done.2, bf16[8,8,64,128]{3,2,1,0:T(8,128)(2,1)S(1)} %copy-done.3, f32[8,8,128]{2,1,0:T(8,128)S(1)} %copy-done.5, ...), custom_call_target="tpu_custom_call" | custom-call | tf_op jit(solution)/shard_map/aggregate_edges/pallas_call | solution.py:283
  62.4 0.0 copy-start
  62.4 0.8 copy-done
  63.2 19.2 %combine_partials.1 = bf16[128,256]{1,0:T(8,128)(2,1)} custom-call(bf16[8,272,128]{2,1,0:T(8,128)(2,1)} %copy-done, bf16[128,128]{1,0:T(8,128)(2,1)} %x_ref.3, bf16[128,256]{1,0:T(8,128)(2,1)} %w_ref.5, f32[1,256]{1,0:T(1,128)} %bitcast.8, f32[1,256]{1,0:T(1,128)} %bitcast.12, f32[1,256]{1,0:T(1,128)} %bitcast.13), custom_call_target="tpu_custom_call" | custom-call | tf_op jit(solution)/shard_map/combine_partials/pallas_call | solution.py:338
  82.4 1.5 %copy.10 = bf16[128,256]{1,0:T(8,128)(2,1)} copy(bf16[128,256]{1,0:T(8,128)(2,1)} %combine_partials.1) | data formatting | bytes 131072
Async XLA Ops:
  37.8 1.6 %copy-start.1 = (s32[1,8,32,16,128]{4,3,2,1,0:T(8,128)S(1)}, s32[1,8,32,16,128]{4,3,2,1,0:T(8,128)}, u32[]{:S(2)}) copy-start(s32[1,8,32,16,128]{4,3,2,1,0:T(8,128)} %param.15) | copy-start | bytes 6291460
  39.4 1.2 %copy-start.2 = (bf16[8,8,64,128]{3,2,1,0:T(8,128)(2,1)S(1)}, bf16[8,8,64,128]{3,2,1,0:T(8,128)(2,1)}, u32[]{:S(2)}) copy-start(bf16[8,8,64,128]{3,2,1,0:T(8,128)(2,1)} %get-tuple-element.8.ga_ref) | copy-start | bytes 3145732
  40.6 1.2 %copy-start.3 = (bf16[8,8,64,128]{3,2,1,0:T(8,128)(2,1)S(1)}, bf16[8,8,64,128]{3,2,1,0:T(8,128)(2,1)}, u32[]{:S(2)}) copy-start(bf16[8,8,64,128]{3,2,1,0:T(8,128)(2,1)} %get-tuple-element.9.gb_ref) | copy-start | bytes 3145732
  41.9 0.8 %copy-start.4 = (bf16[128,256]{1,0:T(8,128)(2,1)S(1)}, bf16[128,256]{1,0:T(8,128)(2,1)}, u32[]{:S(2)}) copy-start(bf16[128,256]{1,0:T(8,128)(2,1)} %w_ref.5) | copy-start | bytes 196612
  42.7 0.8 copy-start.5
  43.5 0.7 copy-start.6
  44.1 0.7 copy-start.7
  44.8 0.7 copy-start.8
  62.4 0.8 copy-start

commit v2 on v1

--- a/solution.py
+++ b/solution.py
@@ -12,25 +12,288 @@
 BLOCK = 128
 HEAD_DIM = 64
 HID = HEADS * HEAD_DIM
-HALF = BLOCK // 2
 SLOPE = 0.2
 RISE = 1.0 - SLOPE
 SAFE = 100.0
 V_ROWS = 80
 P_ROWS = HID + 16
+OPEN = float(jnp.finfo(jnp.bfloat16).max)
+HALF = BLOCK // 2
+SUM_ROWS = HID + 16
 GROUP = 4
 MESH = pl.DeviceIdType.MESH
 F32 = jnp.float32
 BF16 = jnp.bfloat16
 NT = (((1,), (1,)), ((), ()))
-TN = (((0,), (0,)), ((), ()))
-
-
-def leaky_relu(raw):
-    return jnp.where(raw > 0, raw, SLOPE * raw)
-
-
-def attention_rows(att):
+
+
+def leaky_relu(raw_score):
+    return jnp.where(raw_score > 0, raw_score, SLOPE * raw_score)
+
+
+def attention_rows(att_src, att_dst):
+    row = lax.broadcasted_iota(jnp.int32, (32, HID), 0)
+    column = lax.broadcasted_iota(jnp.int32, (32, HID), 1)
+    att = jnp.where(row % 8 < HEADS, att_src, att_dst)
+    high = att.astype(BF16).astype(F32)
+    middle = (att - high).astype(BF16).astype(F32)
+    low = att - high - middle
+    piece = jnp.where(row < 8, high, jnp.where(row < 16, middle, low))
+    return jnp.where((row % HEADS == column // HEAD_DIM) & (row < 24), piece, 0.0).astype(BF16)
+
+
+def scores_of(rows, projected_t):
+    parts = jnp.dot(rows, projected_t, preferred_element_type=F32)
+    return parts[0:8] + parts[8:16] + parts[16:24]
+
+
+def project_t(weight_t, feats):
+    return lax.dot_general(weight_t, feats, NT, preferred_element_type=F32).astype(BF16)
+
+
+def layer_kernel(side, cols, src_ref, count_ref, x_any, w_any, asrc_any, adst_any, bias_any, bits_any, out_ref, peak_ref,
+                 x_ref, w_ref, asrc_ref, adst_ref, bias_ref, bits, feats, dme, dall, wt, rows, vt, eb, mask, parts, land,
+                 own_total, own_weight, load_sem, d_send, d_recv, one_send, one_recv, two_send, two_recv, rs_send, rs_recv):
+    r, c = lax.axis_index("rows"), lax.axis_index("cols")
+    y, z = r // side, r % side
+    quarter = side // 2
+    links = bits.shape[1]
+
+    def at(yy, zz):
+        return (yy * side + zz, c)
+
+    barrier = pltpu.get_barrier_semaphore()
+    for k in range(1, side):
+        pl.semaphore_signal(barrier, inc=1, device_id=at(y, (z + k) % side), device_id_type=MESH)
+        pl.semaphore_signal(barrier, inc=1, device_id=at((y + k) % side, z), device_id_type=MESH)
+    for k in range(1, cols):
+        pl.semaphore_signal(barrier, inc=1, device_id=(r, (c + k) % cols), device_id_type=MESH)
+
+    loads = [
+        pltpu.make_async_copy(a, b, load_sem.at[i])
+        for i, (a, b) in enumerate([
+            (x_any, x_ref), (w_any, w_ref), (asrc_any, asrc_ref), (adst_any, adst_ref), (bias_any, bias_ref),
+            (bits_any, bits)])
+    ]
+    for copy in loads:
+        copy.start()
+    for copy in loads[:4]:
+        copy.wait()
+
+    odd = (y + z) % 2
+    block = jnp.where(odd == 0, y, z)
+    index = jnp.where(odd == 0, z, y) // 2
+    place = lax.broadcasted_iota(jnp.int32, (BLOCK, BLOCK), 0)
+    node = lax.broadcasted_iota(jnp.int32, (BLOCK, BLOCK), 1)
+    order = jnp.where(node == 8 * (place % 16) + place // 16, 1.0, 0.0).astype(BF16)
+    feats[odd, block, index] = jnp.dot(order, x_ref[...], preferred_element_type=F32).astype(BF16)
+
+    pl.semaphore_wait(barrier, 2 * (side - 1) + cols - 1)
+    first = []
+    for k in range(1, side):
+        peer = at(jnp.where(odd == 0, y, (y + k) % side), jnp.where(odd == 0, (z + k) % side, z))
+        mine = feats.at[odd, block, index]
+        first.append(pltpu.make_async_remote_copy(
+            mine, mine, one_send.at[k - 1], one_recv.at[k - 1], device_id=peer, device_id_type=MESH))
+        first[-1].start()
+
+    wt[...] = jnp.transpose(w_ref[...].astype(F32)).astype(BF16)
+    rows[...] = attention_rows(asrc_ref[...], adst_ref[...])
+    projected = project_t(wt[...], x_ref[...])
+    own_score = scores_of(rows[...], projected)
+    dme[...] = jnp.concatenate([own_score[HEADS:], own_score[:HEADS]], axis=0)
+    scores = []
+    for k in range(1, cols):
+        scores.append(pltpu.make_async_remote_copy(
+            dme, dall.at[c], d_send.at[k - 1], d_recv.at[k - 1],
+            device_id=(r, (c + k) % cols), device_id_type=MESH))
+        scores[-1].start()
+    dall[c] = dme[...]
+    raw = own_score[:HEADS] + own_score[HEADS:]
+    self_weight = jnp.exp(leaky_relu(raw)).astype(BF16).astype(F32)
+    own_weight[...] = jnp.concatenate([self_weight, jnp.zeros_like(self_weight)], axis=0)
+    own_total[...] = jnp.concatenate(
+        [projected[h * HEAD_DIM:(h + 1) * HEAD_DIM].astype(F32) * self_weight[h:h + 1] for h in range(HEADS)], axis=0)
+
+    for copy in loads[4:]:
+        copy.wait()
+
+    def unpack(i, carry):
+        d, slot = i // links, i % links
+        live = jnp.where(slot < count_ref[0, d], 1, 0)
+        words = (bits[d, slot] * live).astype(jnp.int16)
+        for k in range(8):
+            mask[d, slot, pl.ds(16 * k, 16)] = jnp.where(
+                (words & (1 << k)) != 0, jnp.asarray(OPEN, BF16), jnp.asarray(0.0, BF16))
+        return carry
+
+    lax.fori_loop(0, bits.shape[0] * links, unpack, 0, unroll=4)
+
+    for copy in first:
+        copy.wait_recv()
+
+    def second(half, way, stage):
+        me = y if half == 0 else z
+        hop = (1 if stage % 2 == 0 else 2) * (1 if way == 0 else -1)
+        back = 0 if stage < 2 else (2 if way == 0 else -2)
+        where = (me - back + side) % side
+        if stage < 3:
+            ref = feats.at[half, where]
+        else:
+            ref = feats.at[half, where, pl.ds(way * (quarter // 2), quarter // 2)]
+        target = (me + hop + side) % side
+        return pltpu.make_async_remote_copy(
+            ref, ref, two_send.at[half, way, stage], two_recv.at[half, way, stage],
+            device_id=at(target, z) if half == 0 else at(y, target), device_id_type=MESH)
+
+    lanes = [(half, way) for half in range(2) for way in range(2)]
+    sent = {(half, way, stage): second(half, way, stage) for stage in range(4) for half, way in lanes}
+    for stage in (1, 0):
+        for half, way in lanes:
+            sent[half, way, stage].start()
+
+    one_row = jnp.where(lax.broadcasted_iota(jnp.int32, (16, BLOCK), 0) == 0, 1.0, 0.0).astype(BF16)
+
+    def prepare(half, where, largest):
+        group = jnp.concatenate([feats[half, where, i] for i in range(quarter)], axis=0)
+        values = project_t(wt[...], group)
+        score = scores_of(rows[...], values)
+        scale = jnp.exp(SLOPE * score).astype(BF16)
+        rise = jnp.exp(RISE * score)
+        for i in range(quarter):
+            lane = slice(i * BLOCK, (i + 1) * BLOCK)
+            across = 2 * i + (where + half) % 2
+            source = jnp.where(half == 0, where * side + across, across * side + where)
+            for h in range(HEADS):
+                row = scale[h:h + 1, lane]
+                vt[source, pl.ds(h * V_ROWS, HEAD_DIM)] = values[h * HEAD_DIM:(h + 1) * HEAD_DIM, lane] * row
+                vt[source, pl.ds(h * V_ROWS + HEAD_DIM, 16)] = one_row * row
+            column = jnp.transpose(rise[:, lane])
+            for h in range(HEADS):
+                eb[source, h] = jnp.broadcast_to(column[:, h:h + 1], (BLOCK, BLOCK)).astype(BF16)
+        return jnp.maximum(largest, jnp.abs(score))
+
+    def near(i, distance, largest):
+        half, way = i // 2, i % 2
+        me = jnp.where(half == 0, y, z)
+        return prepare(half, (me + jnp.where(way == 0, -distance, distance) + side) % side, largest)
+
+    largest = jnp.zeros((8, quarter * BLOCK), F32)
+    largest = lax.fori_loop(0, 2, lambda i, m: near(2 * i, 0, m), largest)
+    for half, way in lanes:
+        sent[half, way, 1].wait_recv()
+        sent[half, way, 2].start()
+        sent[half, way, 3].start()
+    for half, way in lanes:
+        sent[half, way, 0].wait_recv()
+    largest = lax.fori_loop(0, 8, lambda i, m: near(i % 4, 1 + i // 4, m), largest)
+    for half, way in lanes:
+        sent[half, way, 2].wait_recv()
+    largest = lax.fori_loop(0, 4, lambda i, m: near(i, 3, m), largest)
+    for half, way in lanes:
+        sent[half, way, 3].wait_recv()
+    largest = lax.fori_loop(0, 2, lambda i, m: near(2 * i, 4, m), largest)
+    for copy in scores:
+        copy.wait_recv()
+    peak = jnp.broadcast_to(jnp.max(largest, axis=(0, 1), keepdims=True), (8, BLOCK))
+
+    def send(k, d):
+        return pltpu.make_async_remote_copy(
+            parts.at[d], land.at[k - 1], rs_send.at[k - 1], rs_recv.at[k - 1], device_id=(r, d), device_id_type=MESH)
+
+    def one_target(k, carry):
+        d = (c + k) % cols
+        target = dall[d]
+        reach = jnp.exp(RISE * target).astype(BF16)
+        fall = jnp.exp(SLOPE * target)
+        sources = [src_ref[d, slot] for slot in range(links)]
+        denominators = []
+        for pair in range(HEADS // 2):
+            weights = []
+            for h in (2 * pair, 2 * pair + 1):
+                mine = jnp.broadcast_to(reach[h:h + 1], (BLOCK, BLOCK))
+                weights.append(jnp.concatenate([
+                    jnp.minimum(jnp.maximum(eb[source, h] * mine, jnp.asarray(1.0, BF16)), mask[d, slot])
+                    for slot, source in enumerate(sources)], axis=0))
+            edge = jnp.concatenate(weights, axis=1)
+            values = jnp.concatenate([vt[source, pl.ds(2 * pair * V_ROWS, 2 * V_ROWS)] for source in sources], axis=1)
+            both = jnp.dot(values, edge, preferred_element_type=F32)
+            for j in range(2):
+                h = 2 * pair + j
+                total = both[j * V_ROWS:(j + 1) * V_ROWS, j * BLOCK:(j + 1) * BLOCK] * fall[h:h + 1]
+                parts[d, pl.ds(h * HEAD_DIM, HEAD_DIM)] = total[:HEAD_DIM].astype(BF16)
+                denominators.append(total[HEAD_DIM:HEAD_DIM + 1])
+        denominators += [jnp.zeros((8 - HEADS, BLOCK), F32), peak]
+        parts[d, pl.ds(HID, 16)] = jnp.concatenate(denominators, axis=0).astype(BF16)
+
+        @pl.when(k < cols)
+        def _():
+            send(k, d).start()
+
+        return carry
+
+    lax.fori_loop(1, cols + 1, one_target, 0)
+
+    total = own_total[...] + parts[c, pl.ds(0, HID)].astype(F32)
+    tail = parts[c, pl.ds(HID, 16)].astype(F32)
+    denominator, peak = own_weight[...] + tail[:8], tail[8:]
+    for k in range(1, cols):
+        send(k, (c + k) % cols).wait_recv()
+        total = total + land[k - 1, pl.ds(0, HID)].astype(F32)
+        tail = land[k - 1, pl.ds(HID, 16)].astype(F32)
+        denominator, peak = denominator + tail[:8], jnp.maximum(peak, tail[8:])
+    blended = jnp.concatenate(
+        [total[h * HEAD_DIM:(h + 1) * HEAD_DIM] / denominator[h:h + 1] for h in range(HEADS)], axis=0)
+    value = jnp.transpose(blended) + bias_ref[...]
+    out_ref[...] = jnp.where(value > 0, value, jnp.exp(jnp.minimum(value, 0.0)) - 1.0).astype(BF16)
+    peak_ref[0, 0] = jnp.max(peak)
+    for copy in first + scores + list(sent.values()):
+        copy.wait_send()
+    for k in range(1, cols):
+        send(k, (c + k) % cols).wait_send()
+
+
+def layer(side, cols, node_feats, weight, att_src, att_dst, out_bias, block_src, block_count, block_bits):
+    vmem = pl.BlockSpec(memory_space=pltpu.VMEM)
+    smem = pl.BlockSpec(memory_space=pltpu.SMEM)
+    hbm = pl.BlockSpec(memory_space=pl.ANY)
+    dma = pltpu.SemaphoreType.DMA
+    sources = side * side
+    dest, links = block_src.shape
+    return pl.pallas_call(
+        functools.partial(layer_kernel, side, cols),
+        out_shape=(jax.ShapeDtypeStruct((BLOCK, HID), BF16), jax.ShapeDtypeStruct((1, 1), F32)),
+        in_specs=[smem, smem] + [hbm] * 6,
+        out_specs=(vmem, smem),
+        scratch_shapes=[
+            pltpu.VMEM((BLOCK, BLOCK), BF16),
+            pltpu.VMEM((BLOCK, HID), BF16),
+            pltpu.VMEM((1, HID), F32),
+            pltpu.VMEM((1, HID), F32),
+            pltpu.VMEM((1, HID), F32),
+            pltpu.VMEM(block_bits.shape, jnp.int32),
+            pltpu.VMEM((2, side, side // 2, BLOCK, BLOCK), BF16),
+            pltpu.VMEM((8, BLOCK), F32),
+            pltpu.VMEM((cols, 8, BLOCK), F32),
+            pltpu.VMEM((HID, BLOCK), BF16),
+            pltpu.VMEM((32, HID), BF16),
+            pltpu.VMEM((sources, HEADS * V_ROWS, BLOCK), BF16),
+            pltpu.VMEM((sources, HEADS, BLOCK, BLOCK), BF16),
+            pltpu.VMEM((dest, links, BLOCK, BLOCK), BF16),
+            pltpu.VMEM((cols, P_ROWS, BLOCK), BF16),
+            pltpu.VMEM((cols - 1, P_ROWS, BLOCK), BF16),
+            pltpu.VMEM((HID, BLOCK), F32),
+            pltpu.VMEM((8, BLOCK), F32),
+            dma((6,)), dma((cols - 1,)), dma((cols - 1,)), dma((side - 1,)), dma((side - 1,)),
+            dma((2, 2, 4)), dma((2, 2, 4)), dma((cols - 1,)), dma((cols - 1,)),
+        ],
+        compiler_params=pltpu.CompilerParams(
+            collective_id=0, has_side_effects=True, vmem_limit_bytes=56 * 1024 * 1024),
+        name="attention_layer",
+    )(block_src, block_count, node_feats, weight, att_src, att_dst, out_bias, block_bits)
+
+
+def vector_rows(att):
     high = att.astype(BF16).astype(F32)
     middle = (att - high).astype(BF16).astype(F32)
     low = att - high - middle
@@ -40,15 +303,6 @@
     return jnp.where((row % 8 == column // HEAD_DIM) & (row < 24), piece, 0.0).astype(BF16)
 
 
-def scores_of(rows, projected_t):
-    parts = jnp.dot(rows, projected_t, preferred_element_type=F32)
-    return parts[0:8] + parts[8:16] + parts[16:24]
-
-
-def project_t(weight_t, feats):
-    return lax.dot_general(weight_t, feats, NT, preferred_element_type=F32).astype(BF16)
-
-
 def transposed(weight):
     return jnp.transpose(weight.astype(F32)).astype(BF16)
 
@@ -72,7 +326,7 @@
     node = lax.broadcasted_iota(jnp.int32, (BLOCK, BLOCK), 1)
     order = jnp.where(node == 8 * (place % 16) + place // 16, 1.0, 0.0).astype(BF16)
     xp[...] = jnp.dot(order, x_ref[...], preferred_element_type=F32).astype(BF16)
-    dme[...] = scores_of(attention_rows(adst_ref[...]), project_t(transposed(w_ref[...]), x_ref[...]))
+    dme[...] = scores_of(vector_rows(adst_ref[...]), project_t(transposed(w_ref[...]), x_ref[...]))
     pl.semaphore_wait(barrier, 2 * (side - 1) + cols - 1)
 
     first = []
@@ -155,20 +409,17 @@
             dma((2, side - 1)), dma((2, side - 1)),
             dma((2, 2, side // 2, 2)), dma((2, 2, side // 2, 2)),
         ],
-        compiler_params=pltpu.CompilerParams(collective_id=0, has_side_effects=True),
+        compiler_params=pltpu.CompilerParams(collective_id=1, has_side_effects=True),
         name="gather_features",
     )(node_feats, weight, att_dst)
 
 
 def aggregate_kernel(side, src_ref, count_ref, bits_ref, ga_ref, gb_ref, d_ref, w_ref, asrc_ref, p_ref,
-                     vt, eb, st, acc):
+                     vt, st, acc):
     dest = d_ref.shape[0]
     weight_t = transposed(w_ref[...])
-    rows = attention_rows(asrc_ref[...])
+    rows = vector_rows(asrc_ref[...])
     ones_row = jnp.where(lax.broadcasted_iota(jnp.int32, (16, BLOCK), 0) == 0, 1.0, 0.0)
-    spread_row = lax.broadcasted_iota(jnp.int32, (16, HEADS * BLOCK), 0)
-    spread_col = lax.broadcasted_iota(jnp.int32, (16, HEADS * BLOCK), 1)
-    spread = jnp.where(spread_row == spread_col // BLOCK, 1.0, 0.0).astype(BF16)
 
     def blocks_of(y):
         pieces = []
@@ -177,27 +428,6 @@
         feats = jnp.concatenate(pieces, axis=0)
         projected = project_t(weight_t, feats)
         return projected, scores_of(rows, projected)
-
-    def prepare(y, largest):
-        projected, score = blocks_of(y)
-        scale = jnp.exp(SLOPE * score)
-        rise = jnp.exp(RISE * score)
-        rise = jnp.concatenate([rise, jnp.zeros_like(rise)], axis=0).astype(BF16)
-        for z in range(side):
-            at = slice(z * BLOCK, (z + 1) * BLOCK)
-            block = y * side + z
-            for h in range(HEADS):
-                c_row = scale[h:h + 1, at]
-                values = projected[h * HEAD_DIM:(h + 1) * HEAD_DIM, at].astype(F32) * c_row
-                vt[block, h] = jnp.concatenate([values, ones_row * c_row], axis=0).astype(BF16)
-            source = lax.dot_general(rise[:, at], spread, TN, preferred_element_type=F32).astype(BF16)
-            for h in range(HEADS):
-                eb[block, pl.ds(h * BLOCK, BLOCK)] = source[:, h * BLOCK:(h + 1) * BLOCK]
-        return jnp.maximum(largest, jnp.abs(score))
-
-    largest = lax.fori_loop(0, side, prepare, jnp.zeros((8, side * BLOCK), F32))
-    largest = jnp.maximum(jnp.max(largest), jnp.max(jnp.abs(d_ref[...])))
-    safe = largest <= SAFE
 
     def run(weights_of, finish):
         def one_row(d, carry):
@@ -229,26 +459,6 @@
         denominators.append(jnp.zeros((16 - HEADS, BLOCK), F32))
         p_ref[d, pl.ds(HID, 16)] = jnp.concatenate(denominators, axis=0).astype(BF16)
 
-    def factored(d, slot, block, own):
-        words = bits_ref[d, slot].astype(jnp.int16)
-        live = [(words & (1 << k)) != 0 for k in range(8)]
-        reach = jnp.exp(RISE * own).astype(BF16)
-        one = jnp.ones((16, BLOCK), BF16)
-        none = jnp.zeros((16, BLOCK), BF16)
-        result = []
-        for h in range(HEADS):
-            target = jnp.broadcast_to(reach[h:h + 1, :], (16, BLOCK))
-            pieces = []
-            for k in range(8):
-                source = eb[block, pl.ds(h * BLOCK + k * 16, 16)]
-                pieces.append(jnp.where(live[k], jnp.maximum(source * target, one), none))
-            result.append(pieces)
-        return result
-
-    @pl.when(safe)
-    def _():
-        run(factored, lambda d, own: store(d, jnp.exp(SLOPE * own)))
-
     def direct(d, slot, block, own):
         words = bits_ref[d, slot]
         live = jnp.concatenate([jnp.right_shift(words, k) & 1 for k in range(8)], axis=0) != 0
@@ -258,21 +468,19 @@
             result.append([jnp.where(live, jnp.exp(leaky_relu(raw)), 0.0).astype(BF16)])
         return result
 
-    @pl.when(jnp.logical_not(safe))
-    def _():
-        def prepare_direct(y, carry):
-            projected, score = blocks_of(y)
-            for z in range(side):
-                at = slice(z * BLOCK, (z + 1) * BLOCK)
-                block = y * side + z
-                for h in range(HEADS):
-                    values = projected[h * HEAD_DIM:(h + 1) * HEAD_DIM, at].astype(F32)
-                    vt[block, h] = jnp.concatenate([values, ones_row], axis=0).astype(BF16)
-                st[block] = jnp.transpose(score[:, at])
-            return carry
-
-        lax.fori_loop(0, side, prepare_direct, 0)
-        run(direct, lambda d, own: store(d, jnp.ones_like(own)))
+    def prepare_direct(y, carry):
+        projected, score = blocks_of(y)
+        for z in range(side):
+            at = slice(z * BLOCK, (z + 1) * BLOCK)
+            block = y * side + z
+            for h in range(HEADS):
+                values = projected[h * HEAD_DIM:(h + 1) * HEAD_DIM, at].astype(F32)
+                vt[block, h] = jnp.concatenate([values, ones_row], axis=0).astype(BF16)
+            st[block] = jnp.transpose(score[:, at])
+        return carry
+
+    lax.fori_loop(0, side, prepare_direct, 0)
+    run(direct, lambda d, own: store(d, jnp.ones_like(own)))
 
 
 def aggregate(side, block_src, block_count, block_bits, ga, gb, target_scores, weight, att_src):
@@ -282,12 +490,11 @@
     sources = side * side
     return pl.pallas_call(
         functools.partial(aggregate_kernel, side),
-        out_shape=jax.ShapeDtypeStruct((dest, P_ROWS, BLOCK), BF16),
+        out_shape=jax.ShapeDtypeStruct((dest, SUM_ROWS, BLOCK), BF16),
         in_specs=[smem, smem, vmem, vmem, vmem, vmem, vmem, vmem],
         out_specs=vmem,
         scratch_shapes=[
             pltpu.VMEM((sources, HEADS, V_ROWS, BLOCK), BF16),
-            pltpu.VMEM((sources, HEADS * BLOCK, BLOCK), BF16),
             pltpu.VMEM((sources, BLOCK, 8), F32),
             pltpu.VMEM((HEADS, V_ROWS, BLOCK), F32),
         ],
@@ -311,7 +518,7 @@
         copies[-1].start()
 
     projected = project_t(transposed(w_ref[...]), x_ref[...])
-    raw = scores_of(attention_rows(asrc_ref[...]), projected) + scores_of(attention_rows(adst_ref[...]), projected)
+    raw = scores_of(vector_rows(asrc_ref[...]), projected) + scores_of(vector_rows(adst_ref[...]), projected)
     self_weight = jnp.exp(leaky_relu(raw)).astype(BF16).astype(F32)
     own = p_ref[c].astype(F32)
     numerator = [
@@ -341,21 +548,29 @@
         in_specs=[vmem] * 6,
         out_specs=vmem,
         scratch_shapes=[
-            pltpu.VMEM((cols - 1, P_ROWS, BLOCK), BF16),
+            pltpu.VMEM((cols - 1, SUM_ROWS, BLOCK), BF16),
             pltpu.SemaphoreType.DMA((cols - 1,)),
             pltpu.SemaphoreType.DMA((cols - 1,)),
         ],
-        compiler_params=pltpu.CompilerParams(collective_id=1, has_side_effects=True),
+        compiler_params=pltpu.CompilerParams(collective_id=2, has_side_effects=True),
         name="combine_partials",
     )(partials, node_feats, weight, att_src, att_dst, out_bias)
 
 
-def shards(side, cols, node_feats, weight, att_src, att_dst, out_bias, block_src, block_count, block_bits):
+def direct_shards(side, cols, node_feats, weight, att_src, att_dst, out_bias, block_src, block_count, block_bits):
     att_src, att_dst, out_bias = (v.reshape(1, HID) for v in (att_src, att_dst, out_bias))
     ga, gb, target_scores = gather(side, cols, node_feats, weight, att_dst)
     partials = aggregate(
         side, block_src[0], block_count[0], block_bits[0], ga, gb, target_scores, weight, att_src)
     return combine(cols, partials, node_feats, weight, att_src, att_dst, out_bias)
+
+
+def shards(side, cols, *args):
+    node_feats, weight, att_src, att_dst, out_bias, block_src, block_count, block_bits = args
+    result, peak = layer(
+        side, cols, node_feats, weight, att_src.reshape(1, HID), att_dst.reshape(1, HID), out_bias.reshape(1, HID),
+        block_src[0], block_count, block_bits[0])
+    return lax.cond(peak[0, 0] <= SAFE, lambda *rest: result, functools.partial(direct_shards, side, cols), *args)
 
 
 def solution(mesh):

time: 84.4 us -> 58.5 us (0.69)
  Pallas kernels: 73.9 us -> 56.9 us
  local copies, waits for them, and re-layouts: 9.92 us -> 0.66 us
    pallas_call x3 -> x1, Pallas kernels: 73.9 us -> 56.9 us  [layer(): pl.pallas_call(functools.partial(layer_kernel, side, cols), out_shape=(ja...]
    unnamed x19 -> x17, local copies, waits for them, and re-layouts: 9.92 us -> 0.66 us
where the time goes in v2:
time: 58.5 us; the launch traced here: 58.4 us
  Pallas kernels  56.9 us (97%)
  between operations  0.74 us (1%)
  local copies, waits for them, and re-layouts  0.66 us (1%)
    pallas_call x1, Pallas kernels, layer(): pl.pallas_call(functools.partial(layer_kernel, side, cols), out_shape=(ja...  56.9 us

profile of v2, /device:TPU:1, one launch (start us, length us, event | category | flops | bytes accessed | tf_op | source)
XLA Modules:
  0.0 58.4 jit_solution(12400844898126204302)
XLA Ops:
  0.0 0.0 copy-start.4
  0.0 0.0 copy-start.11
  0.0 0.0 copy-start.7
  0.0 0.0 copy-start.10
  0.0 0.0 copy-start.9
  0.0 0.0 copy-start.8
  0.0 0.0 copy-start.5
  0.0 0.0 copy-start.6
  0.1 56.9 %attention_layer.1 = (bf16[128,256]{1,0:T(8,128)(2,1)S(1)}, f32[1,1]{1,0:T(1,128)}) custom-call(s32[8,32]{1,0:T(8,128)} %bitcast.14, s32[1,8]{1,0:T(1,128)} %count_ref.1, bf16[128,128]{1,0:T(8,128)(2,1)} %x_any.1, bf16[128,256]{1,0:T(8,128)(2,1)} %w_any.1, f32[1,256]{1,0:T(1,128)} %bitcast.16, f32[1,256]{1,0:T(1,128)} %bitcast.19, f32[1,256]{1,0:T(1,128)} %bitcast.22, ...), custom_call_target="tpu_custom_call" | custom-call | tf_op jit(solution)/shard_map/attention_layer/pallas_call | solution.py:263
  57.6 0.0 copy-done.4
  57.6 0.0 copy-done.11
  57.7 0.0 copy-done.7
  57.7 0.0 copy-done.10
  57.7 0.0 copy-done.9
  57.7 0.0 copy-done.8
  57.7 0.0 copy-done.5
  57.7 0.0 copy-done.6
  57.7 0.6 %copy.14 = bf16[128,256]{1,0:T(8,128)(2,1)} copy(bf16[128,256]{1,0:T(8,128)(2,1)S(1)} %get-tuple-element.40) | data formatting | bytes 131072
  (1 shorter events, 0.0 us)
Async XLA Ops:
  0.0 57.6 %copy-start.4 = (s32[1,8,32,16,128]{4,3,2,1,0:T(8,128)S(1)}, s32[1,8,32,16,128]{4,3,2,1,0:T(8,128)}, u32[]{:S(2)}) copy-start(s32[1,8,32,16,128]{4,3,2,1,0:T(8,128)} %param.17) | copy-start | bytes 6291460
  0.0 57.6 %copy-start.11 = (s32[1,8]{1,0:T(1,128)S(1)}, s32[1,8]{1,0:T(1,128)}, u32[]{:S(2)}) copy-start(s32[1,8]{1,0:T(1,128)} %count_ref.1) | copy-start | bytes 100
  0.0 57.7 %copy-start.7 = (s32[1,8,32]{2,1,0:T(8,128)S(1)}, s32[1,8,32]{2,1,0:T(8,128)}, u32[]{:S(2)}) copy-start(s32[1,8,32]{2,1,0:T(8,128)} %param.15) | copy-start | bytes 3076
  0.0 57.7 %copy-start.10 = (f32[256]{0:T(256)S(1)}, f32[256]{0:T(256)}, u32[]{:S(2)}) copy-start(f32[256]{0:T(256)} %param.14) | copy-start | bytes 3076
  0.0 57.7 %copy-start.9 = (f32[256]{0:T(256)S(1)}, f32[256]{0:T(256)}, u32[]{:S(2)}) copy-start(f32[256]{0:T(256)} %param.13) | copy-start | bytes 3076
  0.0 57.7 %copy-start.8 = (f32[256]{0:T(256)S(1)}, f32[256]{0:T(256)}, u32[]{:S(2)}) copy-start(f32[256]{0:T(256)} %param.12) | copy-start | bytes 3076
  0.0 57.7 %copy-start.5 = (bf16[128,256]{1,0:T(8,128)(2,1)S(1)}, bf16[128,256]{1,0:T(8,128)(2,1)}, u32[]{:S(2)}) copy-start(bf16[128,256]{1,0:T(8,128)(2,1)} %w_any.1) | copy-start | bytes 196612
  0.0 57.7 %copy-start.6 = (bf16[128,128]{1,0:T(8,128)(2,1)S(1)}, bf16[128,128]{1,0:T(8,128)(2,1)}, u32[]{:S(2)}) copy-start(bf16[128,128]{1,0:T(8,128)(2,1)} %x_any.1) | copy-start | bytes 98308

commit v3 on v2

--- a/solution.py
+++ b/solution.py
@@ -62,13 +62,6 @@
     def at(yy, zz):
         return (yy * side + zz, c)
 
-    barrier = pltpu.get_barrier_semaphore()
-    for k in range(1, side):
-        pl.semaphore_signal(barrier, inc=1, device_id=at(y, (z + k) % side), device_id_type=MESH)
-        pl.semaphore_signal(barrier, inc=1, device_id=at((y + k) % side, z), device_id_type=MESH)
-    for k in range(1, cols):
-        pl.semaphore_signal(barrier, inc=1, device_id=(r, (c + k) % cols), device_id_type=MESH)
-
     loads = [
         pltpu.make_async_copy(a, b, load_sem.at[i])
         for i, (a, b) in enumerate([
@@ -77,6 +70,14 @@
     ]
     for copy in loads:
         copy.start()
+
+    barrier = pltpu.get_barrier_semaphore()
+    for k in range(1, side):
+        pl.semaphore_signal(barrier, inc=1, device_id=at(y, (z + k) % side), device_id_type=MESH)
+        pl.semaphore_signal(barrier, inc=1, device_id=at((y + k) % side, z), device_id_type=MESH)
+    for k in range(1, cols):
+        pl.semaphore_signal(barrier, inc=1, device_id=(r, (c + k) % cols), device_id_type=MESH)
+
     for copy in loads[:4]:
         copy.wait()
 
@@ -96,6 +97,43 @@
         first.append(pltpu.make_async_remote_copy(
             mine, mine, one_send.at[k - 1], one_recv.at[k - 1], device_id=peer, device_id_type=MESH))
         first[-1].start()
+
+    halves = (odd, 1 - odd)
+    sent = {}
+
+    def along(half, delta):
+        target_y = jnp.where(half == 0, (y + delta + side) % side, y)
+        target_z = jnp.where(half == 0, z, (z + delta + side) % side)
+        return at(target_y, target_z)
+
+    def pass_on(role, way, step, piece):
+        half = halves[role]
+        me, across = jnp.where(half == 0, y, z), jnp.where(half == 0, z, y)
+        sign = 1 if way == 0 else -1
+        origin = (me - sign * (step - 1) + side) % side
+        same = (role + step - 1) % 2 == 0
+        offset = ((0, 2, -2, 4) if same else (1, -1, 3, -3))[piece]
+        ref = feats.at[half, origin, (across + offset + side) % side // 2]
+        copy = pltpu.make_async_remote_copy(
+            ref, ref, two_send.at[half, way, step - 1, piece], two_recv.at[half, way, step - 1, piece],
+            device_id=along(half, sign), device_id_type=MESH)
+        copy.start()
+        sent[role, way, step, piece] = copy
+
+    lanes = [(role, way) for role in range(2) for way in range(2)]
+
+    def forward(step, pieces):
+        for piece in pieces:
+            for role, way in lanes:
+                arrive(role, way, step - 1, piece)
+                if step < side // 2 or piece // 2 == way:
+                    pass_on(role, way, step, piece)
+
+    def arrive(role, way, step, piece):
+        sent[role, way, step, piece].wait_recv()
+
+    for way in range(2):
+        pass_on(0, way, 1, 0)
 
     wt[...] = jnp.transpose(w_ref[...].astype(F32)).astype(BF16)
     rows[...] = attention_rows(asrc_ref[...], adst_ref[...])
@@ -129,28 +167,10 @@
 
     lax.fori_loop(0, bits.shape[0] * links, unpack, 0, unroll=4)
 
-    for copy in first:
-        copy.wait_recv()
-
-    def second(half, way, stage):
-        me = y if half == 0 else z
-        hop = (1 if stage % 2 == 0 else 2) * (1 if way == 0 else -1)
-        back = 0 if stage < 2 else (2 if way == 0 else -2)
-        where = (me - back + side) % side
-        if stage < 3:
-            ref = feats.at[half, where]
-        else:
-            ref = feats.at[half, where, pl.ds(way * (quarter // 2), quarter // 2)]
-        target = (me + hop + side) % side
-        return pltpu.make_async_remote_copy(
-            ref, ref, two_send.at[half, way, stage], two_recv.at[half, way, stage],
-            device_id=at(target, z) if half == 0 else at(y, target), device_id_type=MESH)
-
-    lanes = [(half, way) for half in range(2) for way in range(2)]
-    sent = {(half, way, stage): second(half, way, stage) for stage in range(4) for half, way in lanes}
-    for stage in (1, 0):
-        for half, way in lanes:
-            sent[half, way, stage].start()
+    for role, piece, distance in ((1, 0, 7), (1, 1, 1), (0, 1, 6), (0, 2, 2), (1, 2, 5), (1, 3, 3), (0, 3, 4)):
+        first[distance - 1].wait_recv()
+        for way in range(2):
+            pass_on(role, way, 1, piece)
 
     one_row = jnp.where(lax.broadcasted_iota(jnp.int32, (16, BLOCK), 0) == 0, 1.0, 0.0).astype(BF16)
 
@@ -168,31 +188,38 @@
                 row = scale[h:h + 1, lane]
                 vt[source, pl.ds(h * V_ROWS, HEAD_DIM)] = values[h * HEAD_DIM:(h + 1) * HEAD_DIM, lane] * row
                 vt[source, pl.ds(h * V_ROWS + HEAD_DIM, 16)] = one_row * row
-            column = jnp.transpose(rise[:, lane])
+            column = jnp.transpose(rise[:, lane]).astype(BF16)
             for h in range(HEADS):
-                eb[source, h] = jnp.broadcast_to(column[:, h:h + 1], (BLOCK, BLOCK)).astype(BF16)
+                eb[source, h] = jnp.broadcast_to(column[:, h:h + 1], (BLOCK, BLOCK))
         return jnp.maximum(largest, jnp.abs(score))
 
-    def near(i, distance, largest):
-        half, way = i // 2, i % 2
+    def near(half, distance, largest):
         me = jnp.where(half == 0, y, z)
-        return prepare(half, (me + jnp.where(way == 0, -distance, distance) + side) % side, largest)
+        largest = prepare(half, (me - distance + side) % side, largest)
+        return prepare(half, (me + distance) % side, largest)
 
     largest = jnp.zeros((8, quarter * BLOCK), F32)
-    largest = lax.fori_loop(0, 2, lambda i, m: near(2 * i, 0, m), largest)
-    for half, way in lanes:
-        sent[half, way, 1].wait_recv()
-        sent[half, way, 2].start()
-        sent[half, way, 3].start()
-    for half, way in lanes:
-        sent[half, way, 0].wait_recv()
-    largest = lax.fori_loop(0, 8, lambda i, m: near(i % 4, 1 + i // 4, m), largest)
-    for half, way in lanes:
-        sent[half, way, 2].wait_recv()
-    largest = lax.fori_loop(0, 4, lambda i, m: near(i, 3, m), largest)
-    for half, way in lanes:
-        sent[half, way, 3].wait_recv()
-    largest = lax.fori_loop(0, 2, lambda i, m: near(2 * i, 4, m), largest)
+    forward(2, (0, 1))
+    largest = prepare(0, y, largest)
+    forward(2, (2,))
+    largest = prepare(1, z, largest)
+    forward(2, (3,))
+    for step in (3, 4):
+        distance = step - 2
+        largest = prepare(0, (y - distance + side) % side, largest)
+        forward(step, (0,))
+        largest = prepare(0, (y + distance) % side, largest)
+        forward(step, (1,))
+        largest = prepare(1, (z - distance + side) % side, largest)
+        forward(step, (2,))
+        largest = prepare(1, (z + distance) % side, largest)
+        forward(step, (3,))
+    largest = lax.fori_loop(0, 2, lambda half, m: near(half, 3, m), largest)
+    for role, way in lanes:
+        for piece in (2 * way, 2 * way + 1):
+            arrive(role, way, side // 2, piece)
+    largest = prepare(0, (y + side // 2) % side, largest)
+    largest = prepare(1, (z + side // 2) % side, largest)
     for copy in scores:
         copy.wait_recv()
     peak = jnp.broadcast_to(jnp.max(largest, axis=(0, 1), keepdims=True), (8, BLOCK))
@@ -285,7 +312,7 @@
             pltpu.VMEM((HID, BLOCK), F32),
             pltpu.VMEM((8, BLOCK), F32),
             dma((6,)), dma((cols - 1,)), dma((cols - 1,)), dma((side - 1,)), dma((side - 1,)),
-            dma((2, 2, 4)), dma((2, 2, 4)), dma((cols - 1,)), dma((cols - 1,)),
+            dma((2, 2, side // 2, side // 2)), dma((2, 2, side // 2, side // 2)), dma((cols - 1,)), dma((cols - 1,)),
         ],
         compiler_params=pltpu.CompilerParams(
             collective_id=0, has_side_effects=True, vmem_limit_bytes=56 * 1024 * 1024),

time: 58.5 us -> 53.5 us (0.915)
  Pallas kernels: 56.9 us -> 51.9 us
    pallas_call x1, Pallas kernels: 56.9 us -> 51.9 us  [layer(): pl.pallas_call(functools.partial(layer_kernel, side, cols), out_shape=(ja...]
where the time goes in v3:
time: 53.5 us; the launch traced here: 53.4 us
  Pallas kernels  51.9 us (97%)
  between operations  0.74 us (1%)
  local copies, waits for them, and re-layouts  0.66 us (1%)
    pallas_call x1, Pallas kernels, layer(): pl.pallas_call(functools.partial(layer_kernel, side, cols), out_shape=(ja...  51.9 us

profile of v3, /device:TPU:1, one launch (start us, length us, event | category | flops | bytes accessed | tf_op | source)
XLA Modules:
  0.0 53.4 jit_solution(8424086308831719111)
XLA Ops:
  0.0 0.0 copy-start.4
  0.0 0.0 copy-start.11
  0.0 0.0 copy-start.7
  0.0 0.0 copy-start.10
  0.0 0.0 copy-start.9
  0.0 0.0 copy-start.8
  0.0 0.0 copy-start.5
  0.0 0.0 copy-start.6
  0.1 51.9 %attention_layer.1 = (bf16[128,256]{1,0:T(8,128)(2,1)S(1)}, f32[1,1]{1,0:T(1,128)}) custom-call(s32[8,32]{1,0:T(8,128)} %bitcast.14, s32[1,8]{1,0:T(1,128)} %count_ref.1, bf16[128,128]{1,0:T(8,128)(2,1)} %x_any.1, bf16[128,256]{1,0:T(8,128)(2,1)} %w_any.1, f32[1,256]{1,0:T(1,128)} %bitcast.16, f32[1,256]{1,0:T(1,128)} %bitcast.19, f32[1,256]{1,0:T(1,128)} %bitcast.22, ...), custom_call_target="tpu_custom_call" | custom-call | tf_op jit(solution)/shard_map/attention_layer/pallas_call | solution.py:290
  52.6 0.0 copy-done.4
  52.6 0.0 copy-done.11
  52.7 0.0 copy-done.7
  52.7 0.0 copy-done.10
  52.7 0.0 copy-done.9
  52.7 0.0 copy-done.8
  52.7 0.0 copy-done.5
  52.7 0.0 copy-done.6
  52.7 0.6 %copy.14 = bf16[128,256]{1,0:T(8,128)(2,1)} copy(bf16[128,256]{1,0:T(8,128)(2,1)S(1)} %get-tuple-element.40) | data formatting | bytes 131072
  (1 shorter events, 0.0 us)
Async XLA Ops:
  0.0 52.6 %copy-start.4 = (s32[1,8,32,16,128]{4,3,2,1,0:T(8,128)S(1)}, s32[1,8,32,16,128]{4,3,2,1,0:T(8,128)}, u32[]{:S(2)}) copy-start(s32[1,8,32,16,128]{4,3,2,1,0:T(8,128)} %param.17) | copy-start | bytes 6291460
  0.0 52.6 %copy-start.11 = (s32[1,8]{1,0:T(1,128)S(1)}, s32[1,8]{1,0:T(1,128)}, u32[]{:S(2)}) copy-start(s32[1,8]{1,0:T(1,128)} %count_ref.1) | copy-start | bytes 100
  0.0 52.6 %copy-start.7 = (s32[1,8,32]{2,1,0:T(8,128)S(1)}, s32[1,8,32]{2,1,0:T(8,128)}, u32[]{:S(2)}) copy-start(s32[1,8,32]{2,1,0:T(8,128)} %param.15) | copy-start | bytes 3076
  0.0 52.7 %copy-start.10 = (f32[256]{0:T(256)S(1)}, f32[256]{0:T(256)}, u32[]{:S(2)}) copy-start(f32[256]{0:T(256)} %param.14) | copy-start | bytes 3076
  0.0 52.7 %copy-start.9 = (f32[256]{0:T(256)S(1)}, f32[256]{0:T(256)}, u32[]{:S(2)}) copy-start(f32[256]{0:T(256)} %param.13) | copy-start | bytes 3076
  0.0 52.7 %copy-start.8 = (f32[256]{0:T(256)S(1)}, f32[256]{0:T(256)}, u32[]{:S(2)}) copy-start(f32[256]{0:T(256)} %param.12) | copy-start | bytes 3076
  0.0 52.7 %copy-start.5 = (bf16[128,256]{1,0:T(8,128)(2,1)S(1)}, bf16[128,256]{1,0:T(8,128)(2,1)}, u32[]{:S(2)}) copy-start(bf16[128,256]{1,0:T(8,128)(2,1)} %w_any.1) | copy-start | bytes 196612
  0.0 52.7 %copy-start.6 = (bf16[128,128]{1,0:T(8,128)(2,1)S(1)}, bf16[128,128]{1,0:T(8,128)(2,1)}, u32[]{:S(2)}) copy-start(bf16[128,128]{1,0:T(8,128)(2,1)} %x_any.1) | copy-start | bytes 98308

commit v4 on v3

--- a/solution.py
+++ b/solution.py
@@ -165,12 +165,18 @@
                 (words & (1 << k)) != 0, jnp.asarray(OPEN, BF16), jnp.asarray(0.0, BF16))
         return carry
 
-    lax.fori_loop(0, bits.shape[0] * links, unpack, 0, unroll=4)
-
-    for role, piece, distance in ((1, 0, 7), (1, 1, 1), (0, 1, 6), (0, 2, 2), (1, 2, 5), (1, 3, 3), (0, 3, 4)):
+    def take(role, piece, distance):
         first[distance - 1].wait_recv()
         for way in range(2):
             pass_on(role, way, 1, piece)
+
+    all_slots = bits.shape[0] * links
+    lax.fori_loop(0, all_slots // 2, unpack, 0, unroll=4)
+    take(1, 0, 7)
+    take(1, 1, 1)
+    lax.fori_loop(all_slots // 2, all_slots, unpack, 0, unroll=4)
+    for role, piece, distance in ((0, 1, 6), (0, 2, 2), (1, 2, 5), (1, 3, 3), (0, 3, 4)):
+        take(role, piece, distance)
 
     one_row = jnp.where(lax.broadcasted_iota(jnp.int32, (16, BLOCK), 0) == 0, 1.0, 0.0).astype(BF16)
 

time: 53.5 us -> 55 us (1.028)
  Pallas kernels: 51.9 us -> 53.4 us
    pallas_call x1, Pallas kernels: 51.9 us -> 53.4 us  [layer(): pl.pallas_call(functools.partial(layer_kernel, side, cols), out_shape=(ja...]
where the time goes in v4:
time: 55 us; the launch traced here: 54.9 us
  Pallas kernels  53.4 us (97%)
  between operations  0.74 us (1%)
  local copies, waits for them, and re-layouts  0.66 us (1%)
    pallas_call x1, Pallas kernels, layer(): pl.pallas_call(functools.partial(layer_kernel, side, cols), out_shape=(ja...  53.4 us

profile of v4, /device:TPU:1, one launch (start us, length us, event | category | flops | bytes accessed | tf_op | source)
XLA Modules:
  0.0 54.9 jit_solution(352455626756515358)
XLA Ops:
  0.0 0.0 copy-start.4
  0.0 0.0 copy-start.11
  0.0 0.0 copy-start.7
  0.0 0.0 copy-start.10
  0.0 0.0 copy-start.9
  0.0 0.0 copy-start.8
  0.0 0.0 copy-start.5
  0.0 0.0 copy-start.6
  0.1 53.4 %attention_layer.1 = (bf16[128,256]{1,0:T(8,128)(2,1)S(1)}, f32[1,1]{1,0:T(1,128)}) custom-call(s32[8,32]{1,0:T(8,128)} %bitcast.14, s32[1,8]{1,0:T(1,128)} %count_ref.1, bf16[128,128]{1,0:T(8,128)(2,1)} %x_any.1, bf16[128,256]{1,0:T(8,128)(2,1)} %w_any.1, f32[1,256]{1,0:T(1,128)} %bitcast.16, f32[1,256]{1,0:T(1,128)} %bitcast.19, f32[1,256]{1,0:T(1,128)} %bitcast.22, ...), custom_call_target="tpu_custom_call" | custom-call | tf_op jit(solution)/shard_map/attention_layer/pallas_call | solution.py:296
  54.1 0.0 copy-done.4
  54.1 0.0 copy-done.11
  54.2 0.0 copy-done.7
  54.2 0.0 copy-done.10
  54.2 0.0 copy-done.9
  54.2 0.0 copy-done.8
  54.2 0.0 copy-done.5
  54.2 0.0 copy-done.6
  54.2 0.6 %copy.14 = bf16[128,256]{1,0:T(8,128)(2,1)} copy(bf16[128,256]{1,0:T(8,128)(2,1)S(1)} %get-tuple-element.40) | data formatting | bytes 131072
  (1 shorter events, 0.0 us)
Async XLA Ops:
  0.0 54.1 %copy-start.4 = (s32[1,8,32,16,128]{4,3,2,1,0:T(8,128)S(1)}, s32[1,8,32,16,128]{4,3,2,1,0:T(8,128)}, u32[]{:S(2)}) copy-start(s32[1,8,32,16,128]{4,3,2,1,0:T(8,128)} %param.17) | copy-start | bytes 6291460
  0.0 54.1 %copy-start.11 = (s32[1,8]{1,0:T(1,128)S(1)}, s32[1,8]{1,0:T(1,128)}, u32[]{:S(2)}) copy-start(s32[1,8]{1,0:T(1,128)} %count_ref.1) | copy-start | bytes 100
  0.0 54.2 %copy-start.7 = (s32[1,8,32]{2,1,0:T(8,128)S(1)}, s32[1,8,32]{2,1,0:T(8,128)}, u32[]{:S(2)}) copy-start(s32[1,8,32]{2,1,0:T(8,128)} %param.15) | copy-start | bytes 3076
  0.0 54.2 %copy-start.10 = (f32[256]{0:T(256)S(1)}, f32[256]{0:T(256)}, u32[]{:S(2)}) copy-start(f32[256]{0:T(256)} %param.14) | copy-start | bytes 3076
  0.0 54.2 %copy-start.9 = (f32[256]{0:T(256)S(1)}, f32[256]{0:T(256)}, u32[]{:S(2)}) copy-start(f32[256]{0:T(256)} %param.13) | copy-start | bytes 3076
  0.0 54.2 %copy-start.8 = (f32[256]{0:T(256)S(1)}, f32[256]{0:T(256)}, u32[]{:S(2)}) copy-start(f32[256]{0:T(256)} %param.12) | copy-start | bytes 3076
  0.0 54.2 %copy-start.5 = (bf16[128,256]{1,0:T(8,128)(2,1)S(1)}, bf16[128,256]{1,0:T(8,128)(2,1)}, u32[]{:S(2)}) copy-start(bf16[128,256]{1,0:T(8,128)(2,1)} %w_any.1) | copy-start | bytes 196612
  0.0 54.2 %copy-start.6 = (bf16[128,128]{1,0:T(8,128)(2,1)S(1)}, bf16[128,128]{1,0:T(8,128)(2,1)}, u32[]{:S(2)}) copy-start(bf16[128,128]{1,0:T(8,128)(2,1)} %x_any.1) | copy-start | bytes 98308
